TPU v7x, 128 devices: a whole 4x4x4 slice. The times are simulated.
128 devices in a mesh: ctx: 32 (over x, z, core), tp: 4 (over y).
Axes of the slice: x: 4, y: 4, z: 4, core: 2. Of those that a mesh axis runs over, the one named last changes fastest.
Arguments:
- projected: float32 [3, 16384, 4096], P(None, 'ctx', 'tp'), may hold values from -6 to 6
- short_filters: float32 [3, 3, 4096], P(None, None, 'tp'), may hold values from -3 to 3
- long_filter: float32 [16384, 4096], P('ctx', 'tp'), may hold values from -1.1 to 1.1, as said below
- skip_gain: float32 [4096], P('tp'), may hold values from -3 to 3
- out_weight: bfloat16 [4096, 4096], P('tp'), may hold values from -0.09375 to 0.09375
Outputs:
- mixer_out: float32 [16384, 4096], P('ctx', 'tp')
Inputs may be any that keep to these rules, and one draw needn't show every extreme that they name: `long_filter`: each channel's filter decays along the tokens; no further structure is promised.
All inputs are finite; a program needn't handle non-finite values.
Results may differ from a plain program's by a relative error of at most 0.0029.
Values sent between devices are 32-bit elements; how exact they have to be, the bound alone decides.
A program may use at most 192 MiB of HBM per device.

v0:
```python
import math

import jax
import jax.numpy as jnp
from jax import lax
from jax.sharding import PartitionSpec as P


def from_behind(block, axis, distance):
    devices = range(lax.axis_size(axis))
    route = [(i - distance, i) for i in devices if i - distance in devices]
    return lax.ppermute(block, axis, route)


def phase_table(row_index, col_index, period, sign):
    product = row_index[:, None] * col_index[None, :] % period
    angle = sign * 2.0 * math.pi / period * product.astype(jnp.float32)
    return (jnp.cos(angle), jnp.sin(angle))


def exact_einsum(form, table, values):
    return jnp.einsum(form, table, values, precision=lax.Precision.HIGHEST)


def complex_rows(table, real_part, imag_part, form):
    cosines, sines = table
    output_real_part = exact_einsum(form, cosines, real_part) - exact_einsum(form, sines, imag_part)
    out_imag = exact_einsum(form, cosines, imag_part) + exact_einsum(form, sines, real_part)
    return (output_real_part, out_imag)


def twist(real_part, imag_part, table):
    cosines = table[0][:, :, None]
    sines = table[1][:, :, None]
    return (real_part * cosines - imag_part * sines, real_part * sines + imag_part * cosines)


def forward_first(blocks, token_positions, period):
    count_blocks = blocks.shape[0]
    freq_rows = jnp.arange(2 * count_blocks, dtype=jnp.int32)
    block_index = jnp.arange(count_blocks, dtype=jnp.int32)
    cosines, sines = phase_table(freq_rows, block_index, 2 * count_blocks, -1.0)
    real_part = exact_einsum("kp,pjc->kjc", cosines, blocks)
    imag_part = exact_einsum("kp,pjc->kjc", sines, blocks)
    return twist(real_part, imag_part, phase_table(freq_rows, token_positions, period, -1.0))


def forward_second(real_part, imag_part):
    inner = jnp.arange(real_part.shape[1], dtype=jnp.int32)
    table = phase_table(inner, inner, real_part.shape[1], -1.0)
    return complex_rows(table, real_part, imag_part, "mj,kjc->kmc")


def inverse_first(real_part, imag_part, freq_positions, period):
    inner = jnp.arange(real_part.shape[1], dtype=jnp.int32)
    table = phase_table(inner, inner, real_part.shape[1], 1.0)
    back_real, inverse_imaginary = complex_rows(table, real_part, imag_part, "jm,kmc->kjc")
    return twist(back_real, inverse_imaginary, phase_table(freq_positions, inner, period, 1.0))


def inverse_second(real_part, imag_part, period):
    freq_count = real_part.shape[0]
    block_index = jnp.arange(freq_count // 2, dtype=jnp.int32)
    freq_rows = jnp.arange(freq_count, dtype=jnp.int32)
    cosines, sines = phase_table(block_index, freq_rows, freq_count, 1.0)
    summed = exact_einsum("pk,kjc->pjc", cosines, real_part) - exact_einsum(
        "pk,kjc->pjc", sines, imag_part
    )
    return summed * (1.0 / period)


def spectrum_product(first_pair, second_pair):
    return (
        first_pair[0] * second_pair[0] - first_pair[1] * second_pair[1],
        first_pair[0] * second_pair[1] + first_pair[1] * second_pair[0],
    )


def per_device(projected, short_filters, long_filter, skip_gain, out_weight):
    length = projected.shape[1]
    rims = from_behind(projected[:, length - 2 :, :], "ctx", 1)
    padded = jnp.concatenate([rims, projected], axis=1)
    tap_zero = short_filters[:, 0][:, None, :] * padded[:, 2 : 2 + length]
    tap_one = short_filters[:, 1][:, None, :] * padded[:, 1 : 1 + length]
    tap_two = short_filters[:, 2][:, None, :] * padded[:, 0:length]
    truncated_filter = tap_zero + tap_one + tap_two
    gated = truncated_filter[1] * truncated_filter[2]
    count_blocks = lax.axis_size("ctx")
    period = 2 * count_blocks * length
    signal, filt = (
        lax.all_to_all(gated[None], "ctx", split_axis=1, concat_axis=0, tiled=True),
        lax.all_to_all(long_filter[None], "ctx", split_axis=1, concat_axis=0, tiled=True),
    )
    position = lax.axis_index("ctx")
    share = length // count_blocks
    token_mine = position * share + jnp.arange(share, dtype=jnp.int32)
    signal_real, signal_imag = forward_first(signal, token_mine, period)
    filter_real, filter_imag = forward_first(filt, token_mine, period)
    moved = (
        lax.all_to_all(signal_real, "ctx", split_axis=0, concat_axis=1, tiled=True),
        lax.all_to_all(signal_imag, "ctx", split_axis=0, concat_axis=1, tiled=True),
        lax.all_to_all(filter_real, "ctx", split_axis=0, concat_axis=1, tiled=True),
        lax.all_to_all(filter_imag, "ctx", split_axis=0, concat_axis=1, tiled=True),
    )
    signal_spec = forward_second(moved[0], moved[1])
    filter_spec = forward_second(moved[2], moved[3])
    product_real, product_imag = spectrum_product(signal_spec, filter_spec)
    freq_mine = position * 2 + jnp.arange(2, dtype=jnp.int32)
    back_real, inverse_imaginary = inverse_first(product_real, product_imag, freq_mine, period)
    whole_real, whole_imag = (
        lax.all_to_all(back_real, "ctx", split_axis=1, concat_axis=0, tiled=True),
        lax.all_to_all(inverse_imaginary, "ctx", split_axis=1, concat_axis=0, tiled=True),
    )
    conv_blocks = inverse_second(whole_real, whole_imag, period)
    conv = lax.all_to_all(conv_blocks, "ctx", split_axis=0, concat_axis=1, tiled=True)[0]
    mixed = conv + skip_gain[None, :] * gated
    gated_out = (truncated_filter[0] * mixed).astype(jnp.bfloat16)
    terms = jnp.dot(gated_out, out_weight, preferred_element_type=jnp.float32)
    return lax.psum_scatter(terms, "tp", scatter_dimension=1, tiled=True)


def solution(mesh):
    return jax.shard_map(
        per_device,
        mesh=mesh,
        in_specs=(
            P(None, "ctx", "tp"),
            P(None, None, "tp"),
            P("ctx", "tp"),
            P("tp"),
            P("tp", None),
        ),
        out_specs=P("ctx", "tp"),
        check_vma=False,
    )
```

profile of v0, /device:TPU:64, one launch (start us, length us, event | category | flops | bytes accessed | tf_op | source)
XLA Modules:
  0.0 789.6 jit_solution(9065823752271356513)
XLA Ops:
  6.5 4.4 broadcast_in_dim.2
  10.9 7.6 all-to-all-start.3
  21.5 17.1 %collective-permute-done = f32[3,2,1024]{2,1,0:T(2,128)S(1)} collective-permute-done((f32[3,2,1024]{2,1,0:T(2,128)S(1)}, f32[3,2,1024]{2,1,0:T(2,128)S(1)}, u32[]{:S(2)}, u32[]{:S(2)}) %collective-permute-start) | collective-permute-done | bytes 24608 | tf_op jit(solution)/shard_map/ppermute | solution.py:12
  38.6 7.7 fusion.3
  53.0 11.8 %all-to-all-start = ((f32[1,512,1024]{2,0,1:T(1,128)}), f32[1,512,1024]{2,0,1:T(1,128)}, u32[]{:S(2)}, u32[]{:S(2)}) async-start(f32[1,512,1024]{2,0,1:T(1,128)} %copy.57), calls=%async_computation | async-start | bytes 4194304 | tf_op jit(solution)/shard_map/all_to_all | solution.py:91
  67.0 6.1 fusion.24
  73.2 18.2 %all-to-all-done = f32[1,512,1024]{2,0,1:T(1,128)} async-done(((f32[1,512,1024]{2,0,1:T(1,128)}), f32[1,512,1024]{2,0,1:T(1,128)}, u32[]{:S(2)}, u32[]{:S(2)}) %all-to-all-start) | async-done | bytes 2097184 | tf_op jit(solution)/shard_map/all_to_all | solution.py:91
  93.5 4.8 fusion.26
  98.3 4.8 fusion.28
  103.1 9.3 %multiply_add_fusion.1 = (f32[64,16,1024]{2,0,1:T(8,128)S(1)}, f32[64,16,1024]{2,0,1:T(8,128)}, f32[64,16,1024]{2,0,1:T(8,128)}, f32[64,16,1024]{2,0,1:T(8,128)}) fusion(f32[64,16,1024]{2,0,1:T(8,128)S(1)} %copy-done.4, f32[64,16]{0,1:T(8,128)S(1)} %get-tuple-element.21, f32[64,16]{0,1:T(8,128)S(1)} %get-tuple-element.20, f32[64,16,1024]{2,0,1:T(8,128)S(1)} %fusion.26, ...), kind=kOutput, calls=%fused_computation.20 | convolution fusion | flops 415264768 | bytes 31465472 | tf_op jit(solution)/shard_map/kp,pjc->kjc/dot_general | solution.py:22
  112.4 4.5 copy.71
  116.9 7.1 all-to-all-start.5
  124.0 6.7 copy.68
  130.7 43.0 %all-to-all-done.5 = f32[64,16,1024]{2,1,0:T(8,128)} async-done(((f32[64,16,1024]{2,1,0:T(8,128)}), f32[64,16,1024]{2,1,0:T(8,128)}, u32[]{:S(2)}, u32[]{:S(2)}) %all-to-all-start.5) | async-done | bytes 4194336 | tf_op jit(solution)/shard_map/all_to_all | solution.py:103
  173.6 9.8 %all-to-all-start.4 = ((f32[64,16,1024]{2,1,0:T(8,128)}), f32[64,16,1024]{2,1,0:T(8,128)}, u32[]{:S(2)}, u32[]{:S(2)}) async-start(f32[64,16,1024]{2,1,0:T(8,128)} %copy.68), calls=%async_computation.4 | async-start | bytes 8388608 | tf_op jit(solution)/shard_map/all_to_all | solution.py:102
  183.4 6.7 copy.63
  190.1 42.9 %all-to-all-done.4 = f32[64,16,1024]{2,1,0:T(8,128)} async-done(((f32[64,16,1024]{2,1,0:T(8,128)}), f32[64,16,1024]{2,1,0:T(8,128)}, u32[]{:S(2)}, u32[]{:S(2)}) %all-to-all-start.4) | async-done | bytes 4194336 | tf_op jit(solution)/shard_map/all_to_all | solution.py:102
  233.0 9.8 %all-to-all-start.2 = ((f32[64,16,1024]{2,1,0:T(8,128)}), f32[64,16,1024]{2,1,0:T(8,128)}, u32[]{:S(2)}, u32[]{:S(2)}) async-start(f32[64,16,1024]{2,1,0:T(8,128)} %copy.63), calls=%async_computation.2 | async-start | bytes 8388608 | tf_op jit(solution)/shard_map/all_to_all | solution.py:101
  242.8 6.6 copy.60
  249.4 43.0 %all-to-all-done.2 = f32[64,16,1024]{2,1,0:T(8,128)} async-done(((f32[64,16,1024]{2,1,0:T(8,128)}), f32[64,16,1024]{2,1,0:T(8,128)}, u32[]{:S(2)}, u32[]{:S(2)}) %all-to-all-start.2) | async-done | bytes 4194336 | tf_op jit(solution)/shard_map/all_to_all | solution.py:101
  292.4 10.0 %all-to-all-start.1 = ((f32[64,16,1024]{2,1,0:T(8,128)}), f32[64,16,1024]{2,1,0:T(8,128)}, u32[]{:S(2)}, u32[]{:S(2)}) async-start(f32[64,16,1024]{2,1,0:T(8,128)} %copy.60), calls=%async_computation.1 | async-start | bytes 8388608 | tf_op jit(solution)/shard_map/all_to_all | solution.py:100
  310.1 17.0 %fusion.40 = f32[2,1024,512]{2,1,0:T(8,128)S(1)} fusion(f32[2,512,1024]{2,1,0:T(8,128)S(1)} %bitcast.133), kind=kOutput, calls=%fused_computation.58 | convolution fusion | flops 6446120960 | bytes 8388608 | tf_op jit(solution)/shard_map/mj,kjc->kmc/dot_general | solution.py:22
  327.1 17.4 %fusion.44 = f32[2,1024,512]{2,1,0:T(8,128)S(1)} fusion(f32[2,512,1024]{2,1,0:T(8,128)S(1)} %bitcast.135), kind=kOutput, calls=%fused_computation.62 | convolution fusion | flops 6446120960 | bytes 8388608 | tf_op jit(solution)/shard_map/mj,kjc->kmc/dot_general | solution.py:22
  344.5 18.3 %fusion.42 = f32[2,1024,512]{2,1,0:T(8,128)} fusion(f32[2,512,1024]{2,1,0:T(8,128)S(1)} %bitcast.131), kind=kOutput, calls=%fused_computation.60 | convolution fusion | flops 6446120960 | bytes 8388608 | tf_op jit(solution)/shard_map/mj,kjc->kmc/dot_general | solution.py:22
  362.8 18.6 %convolution_add_fusion = f32[2,1024,512]{2,1,0:T(8,128)} fusion(f32[2,1024,512]{2,1,0:T(8,128)S(1)} %fusion.40, f32[2,512,1024]{2,1,0:T(8,128)S(1)} %bitcast.136), kind=kOutput, calls=%fused_computation.26 | convolution fusion | flops 6447169536 | bytes 12582912 | tf_op jit(solution)/shard_map/mj,kjc->kmc/dot_general | solution.py:22
  381.4 19.0 %convolution_subtract_fusion = f32[2,1024,512]{2,1,0:T(8,128)} fusion(f32[2,1024,512]{2,1,0:T(8,128)S(1)} %fusion.44, f32[2,512,1024]{2,1,0:T(8,128)S(1)} %bitcast.134), kind=kOutput, calls=%fused_computation.28 | convolution fusion | flops 6447169536 | bytes 12582912 | tf_op jit(solution)/shard_map/mj,kjc->kmc/dot_general | solution.py:22
  402.9 18.0 %fusion.46 = f32[2,1024,512]{2,1,0:T(8,128)S(1)} fusion(f32[2,512,1024]{2,1,0:T(8,128)S(1)} %bitcast.139), kind=kOutput, calls=%fused_computation.64 | convolution fusion | flops 6446120960 | bytes 8388608 | tf_op jit(solution)/shard_map/mj,kjc->kmc/dot_general | solution.py:22
  421.0 18.4 %convolution_subtract_fusion.1 = f32[2,1024,512]{2,1,0:T(8,128)} fusion(f32[2,1024,512]{2,1,0:T(8,128)S(1)} %fusion.46, f32[2,512,1024]{2,1,0:T(8,128)S(1)} %bitcast.132), kind=kOutput, calls=%fused_computation.29 | convolution fusion | flops 6447169536 | bytes 12582912 | tf_op jit(solution)/shard_map/mj,kjc->kmc/dot_general | solution.py:22
  439.4 22.9 %multiply_subtract_fusion = (f32[2,1024,512]{2,1,0:T(8,128)S(1)}, f32[2,1024,512]{2,1,0:T(8,128)S(1)}) fusion(f32[2,1024,512]{2,1,0:T(8,128)S(1)} %copy-done.5, f32[2,1024,512]{2,1,0:T(8,128)} %convolution_subtract_fusion.1, f32[2,1024,512]{2,1,0:T(8,128)} %convolution_subtract_fusion, f32[2,1024,512]{2,1,0:T(8,128)S(1)} %copy-done.3, ...), kind=kOutput, calls=%fused_computation.19 | convolution fusion | flops 6453460992 | bytes 29360128 | tf_op jit(solution)/shard_map/mj,kjc->kmc/dot_general | solution.py:22
  462.3 11.2 %fusion.5 = f32[2,1024,512]{2,1,0:T(8,128)S(1)} fusion(f32[2,1024,512]{2,1,0:T(8,128)S(1)} %get-tuple-element.6), kind=kOutput, calls=%fused_computation.8 | convolution fusion | flops 6446120960 | bytes 8388608 | tf_op jit(solution)/shard_map/jm,kmc->kjc/dot_general | solution.py:22
  473.5 11.1 %fusion.7 = f32[2,1024,512]{2,1,0:T(8,128)S(1)} fusion(f32[2,1024,512]{2,1,0:T(8,128)S(1)} %get-tuple-element.6), kind=kOutput, calls=%fused_computation.10 | convolution fusion | flops 6446120960 | bytes 8388608 | tf_op jit(solution)/shard_map/jm,kmc->kjc/dot_general | solution.py:22
  484.6 11.3 %fusion.13 = f32[2,1024,512]{2,1,0:T(8,128)S(1)} fusion(f32[2,1024,512]{2,1,0:T(8,128)S(1)} %fusion.7, f32[2,1024,512]{2,1,0:T(8,128)S(1)} %get-tuple-element.5), kind=kOutput, calls=%fused_computation.24 | convolution fusion | flops 6447169536 | bytes 12582912 | tf_op jit(solution)/shard_map/jm,kmc->kjc/dot_general | solution.py:22
  495.9 14.0 %add_bitcast_fusion = (f32[2,512,1024]{1,2,0:T(8,128)}, f32[2,512,1024]{1,2,0:T(8,128)}) fusion(f32[2,1024,512]{2,1,0:T(8,128)S(1)} %fusion.13, f32[2,512]{1,0:T(2,128)S(1)} %get-tuple-element.19, f32[2,512]{1,0:T(2,128)S(1)} %get-tuple-element.18, f32[2,1024,512]{2,1,0:T(8,128)S(1)} %fusion.5, f32[2,1024,512]{2,1,0:T(8,128)S(1)} %get-tuple-element.5), kind=kOutput, calls=%fused_computation.16 | convolution fusion | flops 6453460992 | bytes 20979712 | tf_op jit(solution)/shard_map/jm,kmc->kjc/dot_general | solution.py:22
  509.9 7.4 copy.81
  517.3 7.4 all-to-all-start.7
  524.7 7.4 copy.78
  532.1 42.2 %all-to-all-done.7 = f32[2,512,1024]{2,0,1:T(2,128)} async-done(((f32[2,512,1024]{2,0,1:T(2,128)}), f32[2,512,1024]{2,0,1:T(2,128)}, u32[]{:S(2)}, u32[]{:S(2)}) %all-to-all-start.7) | async-done | bytes 4194336 | tf_op jit(solution)/shard_map/all_to_all | solution.py:112
  574.3 9.8 %all-to-all-start.6 = ((f32[2,512,1024]{2,0,1:T(2,128)}), f32[2,512,1024]{2,0,1:T(2,128)}, u32[]{:S(2)}, u32[]{:S(2)}) async-start(f32[2,512,1024]{2,0,1:T(2,128)} %copy.78), calls=%async_computation.6 | async-start | bytes 8388608 | tf_op jit(solution)/shard_map/all_to_all | solution.py:111
  584.2 3.5 copy.82
  587.7 5.3 copy.83
  593.0 6.3 all_to_all.130
  599.3 34.4 %all-to-all-done.6 = f32[2,512,1024]{2,0,1:T(2,128)} async-done(((f32[2,512,1024]{2,0,1:T(2,128)}), f32[2,512,1024]{2,0,1:T(2,128)}, u32[]{:S(2)}, u32[]{:S(2)}) %all-to-all-start.6) | async-done | bytes 4194336 | tf_op jit(solution)/shard_map/all_to_all | solution.py:111
  637.2 5.3 copy.80
  642.6 6.0 all_to_all.126
  648.6 4.1 fusion.86
  656.4 36.5 %all_to_all.141 = f32[32,16,1024]{2,1,0:T(8,128)S(1)} all-to-all(f32[32,16,1024]{2,1,0:T(8,128)S(1)} %copy.84), channel_id=1, replica_groups=mesh['ctx'=32,'tp'=4] {'ctx'}, dimensions={0} | all-to-all | bytes 4194304 | tf_op jit(solution)/shard_map/all_to_all | solution.py:115
  695.1 6.8 fusion.194
  701.9 80.3 %reduce-scatter.2.cloned.1.call-done = f32[512,1024]{1,0:T(8,128)} async-done(((f32[512,4096]{1,0:T(8,128)}), f32[512,1024]{1,0:T(8,128)}) %reduce-scatter.2.cloned.1.call-update) | async-done | bytes 2097168 | tf_op jit(solution)/shard_map/reduce_scatter | solution.py:119
  (55 shorter events, 33.5 us)
Async XLA Ops:
  6.5 14.9 %copy-start.8 = (f32[3,3,1024]{2,1,0:T(4,128)S(1)}, f32[3,3,1024]{2,1,0:T(4,128)}, u32[]{:S(2)}) copy-start(f32[3,3,1024]{2,1,0:T(4,128)} %param.6) | copy-start | bytes 110596
  10.9 42.2 %all-to-all-start.3 = ((f32[1,512,1024]{2,0,1:T(1,128)}), f32[1,512,1024]{2,0,1:T(1,128)S(1)}, u32[]{:S(2)}, u32[]{:S(2)}) async-start(f32[1,512,1024]{2,0,1:T(1,128)} %broadcast_in_dim.2), calls=%async_computation.3 | async-start | bytes 4194304 | tf_op jit(solution)/shard_map/all_to_all | solution.py:92
  19.4 19.2 %collective-permute-start = (f32[3,2,1024]{2,1,0:T(2,128)S(1)}, f32[3,2,1024]{2,1,0:T(2,128)S(1)}, u32[]{:S(2)}, u32[]{:S(2)}) collective-permute-start(f32[3,2,1024]{2,1,0:T(2,128)S(1)} %slice.29), channel_id=1, source_target_pairs={{0,4},{4,8},{8,12},{12,16},{16,20},{20,24},{24,28},{28,32},{32,36}... | collective-permute-start | bytes 73736 | tf_op jit(solution)/shard_map/ppermute | solution.py:12
  46.4 2.7 copy-start.2
  53.0 11.8 %copy-start.7 = (f32[1,512,1024]{2,0,1:T(1,128)}, f32[1,512,1024]{2,0,1:T(1,128)S(1)}, u32[]{:S(2)}) copy-start(f32[1,512,1024]{2,0,1:T(1,128)S(1)} %all-to-all-done.3) | copy-start | bytes 6291460
  53.0 38.4 %all-to-all-start = ((f32[1,512,1024]{2,0,1:T(1,128)}), f32[1,512,1024]{2,0,1:T(1,128)}, u32[]{:S(2)}, u32[]{:S(2)}) async-start(f32[1,512,1024]{2,0,1:T(1,128)} %copy.57), calls=%async_computation | async-start | bytes 4194304 | tf_op jit(solution)/shard_map/all_to_all | solution.py:91
  98.3 4.8 copy-start.4
  116.9 56.7 %all-to-all-start.5 = ((f32[64,16,1024]{2,1,0:T(8,128)}), f32[64,16,1024]{2,1,0:T(8,128)}, u32[]{:S(2)}, u32[]{:S(2)}) async-start(f32[64,16,1024]{2,1,0:T(8,128)} %copy.71), calls=%async_computation.5 | async-start | bytes 8388608 | tf_op jit(solution)/shard_map/all_to_all | solution.py:103
  173.6 59.4 %all-to-all-start.4 = ((f32[64,16,1024]{2,1,0:T(8,128)}), f32[64,16,1024]{2,1,0:T(8,128)}, u32[]{:S(2)}, u32[]{:S(2)}) async-start(f32[64,16,1024]{2,1,0:T(8,128)} %copy.68), calls=%async_computation.4 | async-start | bytes 8388608 | tf_op jit(solution)/shard_map/all_to_all | solution.py:102
  233.0 59.4 %all-to-all-start.2 = ((f32[64,16,1024]{2,1,0:T(8,128)}), f32[64,16,1024]{2,1,0:T(8,128)}, u32[]{:S(2)}, u32[]{:S(2)}) async-start(f32[64,16,1024]{2,1,0:T(8,128)} %copy.63), calls=%async_computation.2 | async-start | bytes 8388608 | tf_op jit(solution)/shard_map/all_to_all | solution.py:101
  292.4 108.0 %all-to-all-start.1 = ((f32[64,16,1024]{2,1,0:T(8,128)}), f32[64,16,1024]{2,1,0:T(8,128)}, u32[]{:S(2)}, u32[]{:S(2)}) async-start(f32[64,16,1024]{2,1,0:T(8,128)} %copy.60), calls=%async_computation.1 | async-start | bytes 8388608 | tf_op jit(solution)/shard_map/all_to_all | solution.py:100
  310.1 34.4 %copy-start = (f32[2,32,16,1024]{3,2,1,0:T(8,128)}, f32[2,32,16,1024]{3,2,1,0:T(8,128)S(1)}, u32[]{:S(2)}) copy-start(f32[2,32,16,1024]{3,2,1,0:T(8,128)S(1)} %copy.64) | copy-start | bytes 12582916
  402.9 18.1 %copy-start.1 = (f32[2,32,16,1024]{3,2,1,0:T(8,128)S(1)}, f32[2,32,16,1024]{3,2,1,0:T(8,128)}, u32[]{:S(2)}) copy-start(f32[2,32,16,1024]{3,2,1,0:T(8,128)} %copy-done) | copy-start | bytes 12582916
  421.0 18.5 %copy-start.3 = (f32[2,1024,512]{2,1,0:T(8,128)S(1)}, f32[2,1024,512]{2,1,0:T(8,128)}, u32[]{:S(2)}) copy-start(f32[2,1024,512]{2,1,0:T(8,128)} %fusion.42) | copy-start | bytes 12582916
  421.0 18.5 %copy-start.5 = (f32[2,1024,512]{2,1,0:T(8,128)S(1)}, f32[2,1024,512]{2,1,0:T(8,128)}, u32[]{:S(2)}) copy-start(f32[2,1024,512]{2,1,0:T(8,128)} %convolution_add_fusion) | copy-start | bytes 12582916
  517.3 57.0 %all-to-all-start.7 = ((f32[2,512,1024]{2,0,1:T(2,128)}), f32[2,512,1024]{2,0,1:T(2,128)}, u32[]{:S(2)}, u32[]{:S(2)}) async-start(f32[2,512,1024]{2,0,1:T(2,128)} %copy.81), calls=%async_computation.7 | async-start | bytes 8388608 | tf_op jit(solution)/shard_map/all_to_all | solution.py:112
  574.3 59.4 %all-to-all-start.6 = ((f32[2,512,1024]{2,0,1:T(2,128)}), f32[2,512,1024]{2,0,1:T(2,128)}, u32[]{:S(2)}, u32[]{:S(2)}) async-start(f32[2,512,1024]{2,0,1:T(2,128)} %copy.78), calls=%async_computation.6 | async-start | bytes 8388608 | tf_op jit(solution)/shard_map/all_to_all | solution.py:111
  584.1 198.1 %reduce-scatter.2.cloned.1.call-start = ((), (), s32[]{:S(2)}) async-start(), calls=%async_computation.10 | async-start | bytes 10485760 | tf_op jit(solution)/shard_map/reduce_scatter | solution.py:119
  648.6 4.1 copy-start.6
  652.8 40.2 %slice-start = ((s8[6291456]{0:T(1024)(128)(4,1)}), s8[4194304]{0:T(1024)(128)(4,1)S(1)}, s32[]{:S(2)}) async-start(s8[6291456]{0:T(1024)(128)(4,1)} %bitcast.137), calls=%async_computation.11 | async-start | bytes 8388608
  655.1 37.8 %slice-start.1 = ((s8[6291456]{0:T(1024)(128)(4,1)}), s8[2097152]{0:T(1024)(128)(4,1)S(1)}, s32[]{:S(2)}) async-start(s8[6291456]{0:T(1024)(128)(4,1)} %bitcast.137), calls=%async_computation.12 | async-start | bytes 4194304
  655.1 37.8 %copy-start.9 = (f32[1024]{0:T(1024)S(1)}, f32[1024]{0:T(1024)}, u32[]{:S(2)}) copy-start(f32[1024]{0:T(1024)} %param.8) | copy-start | bytes 12292
  655.1 38.9 %slice-start.2 = ((s8[8388608]{0:T(1024)(128)(4,1)}), s8[4194304]{0:T(1024)(128)(4,1)S(1)}, s32[]{:S(2)}) async-start(s8[8388608]{0:T(1024)(128)(4,1)} %bitcast.148), calls=%async_computation.13 | async-start | bytes 8388608
  692.9 2.2 slice-start.3
Sparse Core Ops, SparseCore 0:
  702.0 80.1 reduce-scatter.1
where the time goes:
time: 800 us; the launch traced here: 790 us
  waiting for transfers between devices  321 us (40%)
  matrix products  235 us (29%)
  local copies, waits for them, and re-layouts  97.1 us (12%)
  starting transfers between devices  75.3 us (9%)
  blocking collectives  36.5 us (5%)
  between operations  14.4 us (2%)
  other arithmetic  9.64 us (1%)
    dot_general x18, matrix products, exact_einsum(): return jnp.einsum(form, table, values, precision=lax.Precision.HIGHEST)  229 us
    reduce_scatter x1, waiting for transfers between devices, per_device(): return lax.psum_scatter(terms, 'tp', scatter_dimension=1, tiled=True)  80.3 us
    all_to_all x1, waiting for transfers between devices, per_device(): lax.all_to_all(signal_imag, 'ctx', split_axis=0, concat_axis=1, tiled=True)  43 us
    all_to_all x1, waiting for transfers between devices, per_device(): lax.all_to_all(filter_imag, 'ctx', split_axis=0, concat_axis=1, tiled=True)  43 us
    all_to_all x1, waiting for transfers between devices, per_device(): lax.all_to_all(filter_real, 'ctx', split_axis=0, concat_axis=1, tiled=True)  42.9 us
    all_to_all x1, waiting for transfers between devices, per_device(): lax.all_to_all(inverse_imaginary, 'ctx', split_axis=1, concat_axis=0, til...  42.2 us
    all_to_all x1, blocking collectives, per_device(): lax.all_to_all(conv_blocks, 'ctx', split_axis=0, concat_axis=1, tiled=True)  36.5 us
    all_to_all x1, waiting for transfers between devices, per_device(): lax.all_to_all(back_real, 'ctx', split_axis=1, concat_axis=0, tiled=True)  34.4 us
  transfers between devices with their start and end apart: 10, of which 8 were waited for; matrix products, arithmetic and copies ran while one was open for 20% of the time, Pallas kernels for 0%

commit v1 on v0

v1 whole, which is shorter than its diff:
```python
import functools

import jax
import jax.numpy as jnp
import ml_dtypes
import numpy as np
from jax import lax
from jax.experimental import pallas as pl
from jax.experimental.pallas import tpu as pltpu
from jax.sharding import PartitionSpec as P

MESH = pl.DeviceIdType.MESH
BF16 = jnp.bfloat16
F32 = jnp.float32
CTX = 32
TP = 4
OWN = 32
GROUP = 8
CHIP_OFFSETS = (
    (1, 0), (3, 0), (0, 1), (0, 3), (1, 1), (3, 3), (1, 3), (3, 1),
    (2, 0), (0, 2), (2, 1), (2, 3), (1, 2), (3, 2), (2, 2),
)
PEERS = tuple((a, b, d) for a, b in CHIP_OFFSETS for d in (0, 1)) + ((0, 0, 1),)


def split_np(table):
    high = table.astype(ml_dtypes.bfloat16)
    low = (table - high.astype(np.float64)).astype(ml_dtypes.bfloat16)
    return high, low


def tables():
    block = np.arange(32)
    n1 = np.concatenate([2 * block, 2 * block + 1]).astype(np.float64)
    k1 = np.arange(64) + 0.25
    n2 = np.arange(256)
    psi = 2 * np.pi * np.outer(k1, n1) / 64
    high, low = split_np(np.concatenate([np.cos(psi), -np.sin(psi)], 0))
    first = np.concatenate([high, high, low], 1)
    phi = 2 * np.pi * np.outer(k1, n2) / 16384
    twist = np.stack([np.cos(phi), np.sin(phi)]).astype(np.float32)
    theta = 2 * np.pi * (np.outer(n2, n2) % 256) / 256
    cosine, sine = np.cos(theta), np.sin(theta)
    high, low = split_np(np.block([[cosine, -sine], [sine, cosine]]))
    second = np.concatenate([high, high, low], 0)
    high, low = split_np(np.block([[cosine, sine], [-sine, cosine]]))
    back_second = np.concatenate([high, high, low], 0)
    high, low = split_np(np.concatenate([np.cos(psi.T), -np.sin(psi.T)], 1) / 16384)
    back_first = np.concatenate([high, high, low], 1)
    return first, twist, second, back_second, back_first


def split(value):
    high = value.astype(BF16)
    return high, (value - high.astype(F32)).astype(BF16)


def dot(left, right):
    return jnp.dot(left, right, preferred_element_type=F32)


def ctx_peer(me, offset):
    a, b, d = offset
    return (me // 8 + a) % 4 * 8 + (me // 2 + b) % 4 * 2 + (me + d) % 2


def greet_ctx(barrier, me, tp):
    def signal(i, carry):
        pl.semaphore_signal(
            barrier, inc=1, device_id=(lax.rem(me + i, CTX), tp), device_id_type=MESH
        )
        return carry

    lax.fori_loop(1, CTX, signal, 0)


def rows_of(device):
    return pl.ds(pl.multiple_of(device * OWN, OWN), OWN)


def send_all(source, target, me, tp, send_sem, recv_sem, pieces):
    pltpu.make_async_copy(
        source.at[:, rows_of(me), :], target.at[:, rows_of(me), :], recv_sem
    ).start()
    step = source.shape[0] // pieces
    for piece in range(pieces):
        for offset in PEERS:
            peer = ctx_peer(me, offset)
            part = pl.ds(piece * step, step)
            pltpu.make_async_remote_copy(
                src_ref=source.at[part, rows_of(peer), :],
                dst_ref=target.at[part, rows_of(me), :],
                send_sem=send_sem,
                recv_sem=recv_sem,
                device_id=(peer, tp),
                device_id_type=MESH,
            ).start()


def wait_arrived(target, recv_sem):
    pltpu.make_async_copy(target, target, recv_sem).wait()


def wait_sent(source, send_sem):
    away = source.at[:, 0 : (CTX - 1) * OWN, :]
    pltpu.make_async_copy(away, away, send_sem).wait()


def short_conv(projected, halo, short_filters, stream, jb, cols):
    rows = projected[stream, jb * 128 : jb * 128 + 128, cols]
    before = halo[stream, :, cols] if jb == 0 else projected[stream, jb * 128 - 8 : jb * 128, cols]
    longer = jnp.concatenate([before, rows], 0)
    taps = short_filters[stream, :, cols]
    return taps[0:1] * rows + taps[1:2] * longer[7:135] + taps[2:3] * longer[6:134]


def spread_kernel(
    projected, short_filters, long_filter, filt, signal, gated, shortened_q,
    halo, halo_in, filt_t, gated_t, send_sem, recv_sem, halo_send, halo_recv,
):
    me = lax.axis_index("ctx")
    tp = lax.axis_index("tp")
    barrier = pltpu.get_barrier_semaphore()
    greet_ctx(barrier, me, tp)

    def turn_filter(cb, carry):
        cols = pl.ds(pl.multiple_of(cb * 128, 128), 128)
        for jb in range(4):
            filt_t[jb, cols, :] = long_filter[jb * 128 : jb * 128 + 128, cols].T
        return carry

    lax.fori_loop(0, 8, turn_filter, 0)
    pl.semaphore_wait(barrier, CTX - 1)
    edge = pltpu.make_async_remote_copy(
        src_ref=projected.at[:, 504:512, :],
        dst_ref=halo_in,
        send_sem=halo_send,
        recv_sem=halo_recv,
        device_id=(lax.rem(me + 1, CTX), tp),
        device_id_type=MESH,
    )
    edge.start()
    send_all(filt_t, filt, me, tp, send_sem.at[0], recv_sem.at[0], 2)
    edge.wait()
    halo[...] = jnp.where(me > 0, halo_in[...], 0.0)

    def gate(cb, carry):
        cols = pl.ds(pl.multiple_of(cb * 128, 128), 128)
        for jb in range(4):
            key = short_conv(projected, halo, short_filters, 1, jb, cols)
            value = short_conv(projected, halo, short_filters, 2, jb, cols)
            product = key * value
            gated[jb * 128 : jb * 128 + 128, cols] = product
            gated_t[jb, cols, :] = product.T
        return carry

    lax.fori_loop(0, 8, gate, 0)
    send_all(gated_t, signal, me, tp, send_sem.at[1], recv_sem.at[1], 2)

    def query(cb, carry):
        cols = pl.ds(pl.multiple_of(cb * 128, 128), 128)
        for jb in range(4):
            shortened_q[jb * 128 : jb * 128 + 128, cols] = short_conv(
                projected, halo, short_filters, 0, jb, cols
            )
        return carry

    lax.fori_loop(0, 8, query, 0)
    wait_sent(filt_t, send_sem.at[0])
    wait_sent(gated_t, send_sem.at[1])
    wait_arrived(filt, recv_sem.at[0])
    wait_arrived(signal, recv_sem.at[1])


def conv_kernel(
    filt, signal, first, twist, second, back_second, back_first, out, rows, spectrum, inner
):
    cosine, sine = twist[0], twist[1]

    def forward(source, group):
        for i in range(GROUP):
            one = pl.ds(group * GROUP + i, CTX, stride=OWN)
            blocks = [source[jb, one, :] for jb in range(4)]
            high, low = split(
                jnp.concatenate(
                    [jnp.concatenate(blocks[:2], 1), jnp.concatenate(blocks[2:], 1)], 0
                )
            )
            turned = dot(first[...], jnp.concatenate([high, low, high], 0))
            real, imag = turned[:64], turned[64:]
            real_high, real_low = split(real * cosine + imag * sine)
            imag_high, imag_low = split(imag * cosine - real * sine)
            rows[i * 64 : i * 64 + 64, :] = jnp.concatenate(
                [real_high, imag_high, real_low, imag_low, real_high, imag_high], 1
            )
        return dot(rows[...], second[...])

    def group_rows(group):
        return pl.ds(pl.multiple_of(group * GROUP * 64, GROUP * 64), GROUP * 64)

    def filter_step(group, carry):
        spectrum[group_rows(group), :] = forward(filt, group)
        return carry

    lax.fori_loop(0, OWN // GROUP, filter_step, 0)

    def signal_step(group, carry):
        left = forward(signal, group)
        right = spectrum[group_rows(group), :]
        left_real, left_imag = left[:, :256], left[:, 256:]
        right_real, right_imag = right[:, :256], right[:, 256:]
        real_high, real_low = split(left_real * right_real - left_imag * right_imag)
        imag_high, imag_low = split(left_real * right_imag + left_imag * right_real)
        product = jnp.concatenate(
            [real_high, imag_high, real_low, imag_low, real_high, imag_high], 1
        )
        inner[group_rows(group), :] = dot(product, back_second[...])
        return carry

    lax.fori_loop(0, OWN // GROUP, signal_step, 0)

    def back_step(group, carry):
        for i in range(GROUP):
            channel = group * GROUP + i
            both = inner[pl.ds(pl.multiple_of(channel * 64, 64), 64), :]
            real, imag = both[:, :256], both[:, 256:]
            real_high, real_low = split(real * cosine - imag * sine)
            imag_high, imag_low = split(imag * cosine + real * sine)
            result = dot(
                back_first[...],
                jnp.concatenate(
                    [real_high, imag_high, real_low, imag_low, real_high, imag_high], 0
                ),
            )
            for jb in range(4):
                out[jb, pl.ds(channel, CTX, stride=OWN), :] = result[
                    jb // 2 * 32 : jb // 2 * 32 + 32, jb % 2 * 128 : jb % 2 * 128 + 128
                ]
        return carry

    lax.fori_loop(0, OWN // GROUP, back_step, 0)


def project_kernel(
    conv, gated, shortened_q, skip_gain, weight_hbm, out,
    weight, conv_in, gated_out, far, near, far_in, near_in,
    send_sem, recv_sem, far_send, far_recv, near_send, near_recv, weight_sem,
):
    me = lax.axis_index("ctx")
    tp = lax.axis_index("tp")
    barrier = pltpu.get_barrier_semaphore()
    greet_ctx(barrier, me, tp)
    up, down = lax.rem(tp + 1, TP), lax.rem(tp + TP - 1, TP)
    for side in (up, down):
        pl.semaphore_signal(barrier, inc=1, device_id=(me, side), device_id_type=MESH)
    load = pltpu.make_async_copy(weight_hbm, weight, weight_sem)
    load.start()
    pl.semaphore_wait(barrier, CTX + 1)
    for jb in range(4):
        chunk = pl.ds(jb, 1)
        send_all(conv.at[chunk], conv_in.at[chunk], me, tp, send_sem.at[jb], recv_sem.at[jb], 1)
    load.wait()

    def columns(quarter):
        return pl.ds(pl.multiple_of(quarter * 1024, 1024), 1024)

    def to_far(jb, side):
        half = slice(512 * side, 512 * side + 512)
        return pltpu.make_async_remote_copy(
            src_ref=far.at[jb, :, half],
            dst_ref=far_in.at[jb, :, half],
            send_sem=far_send.at[jb, side],
            recv_sem=far_recv.at[jb, side],
            device_id=(me, (up, down)[side]),
            device_id_type=MESH,
        )

    def to_near(jb, side):
        return pltpu.make_async_remote_copy(
            src_ref=near.at[jb, side],
            dst_ref=near_in.at[jb, side],
            send_sem=near_send.at[jb, side],
            recv_sem=near_recv.at[jb, side],
            device_id=(me, (up, down)[side]),
            device_id_type=MESH,
        )

    def compute(jb):
        wait_arrived(conv_in.at[pl.ds(jb, 1)], recv_sem.at[jb])
        tokens = slice(jb * 128, jb * 128 + 128)
        mixed = conv_in[jb].T + skip_gain[...] * gated[tokens, :]
        gated_out[...] = (shortened_q[tokens, :] * mixed).astype(BF16)
        far[jb] = dot(gated_out[...], weight[:, columns(lax.rem(tp + 2, TP))])
        to_far(jb, 0).start()
        to_far(jb, 1).start()
        near[jb, 0] = dot(gated_out[...], weight[:, columns(up)])
        near[jb, 1] = dot(gated_out[...], weight[:, columns(down)])
        out[tokens, :] = dot(gated_out[...], weight[:, columns(tp)])

    def relay(jb):
        for side in (0, 1):
            half = slice(512 * side, 512 * side + 512)
            to_far(jb, side).wait_recv()
            near[jb, side, :, half] += far_in[jb, :, half]
            to_near(jb, side).start()

    compute(0)
    for jb in range(1, 4):
        compute(jb)
        relay(jb - 1)
    relay(3)
    for jb in range(4):
        tokens = slice(jb * 128, jb * 128 + 128)
        to_near(jb, 0).wait_recv()
        to_near(jb, 1).wait_recv()
        out[tokens, :] += near_in[jb, 0] + near_in[jb, 1]
    for jb in range(4):
        wait_sent(conv.at[pl.ds(jb, 1)], send_sem.at[jb])
        for side in (0, 1):
            to_far(jb, side).wait_send()
            to_near(jb, side).wait_send()


VMEM = pl.BlockSpec(memory_space=pltpu.VMEM)
ANY = pl.BlockSpec(memory_space=pl.ANY)
DMA = pltpu.SemaphoreType.DMA


def array(*shape):
    return jax.ShapeDtypeStruct(shape, F32)


def per_device(projected, short_filters, long_filter, skip_gain, out_weight):
    filt, signal, gated, shortened_q = pl.pallas_call(
        spread_kernel,
        out_shape=(array(4, 1024, 128), array(4, 1024, 128), array(512, 1024), array(512, 1024)),
        in_specs=[VMEM] * 3,
        out_specs=(VMEM,) * 4,
        scratch_shapes=[
            pltpu.VMEM((3, 8, 1024), F32),
            pltpu.VMEM((3, 8, 1024), F32),
            pltpu.VMEM((4, 1024, 128), F32),
            pltpu.VMEM((4, 1024, 128), F32),
            DMA((2,)),
            DMA((2,)),
            DMA,
            DMA,
        ],
        compiler_params=pltpu.CompilerParams(
            collective_id=0, has_side_effects=True, vmem_limit_bytes=48 * 2**20
        ),
        name="spread",
    )(projected, short_filters, long_filter)
    conv = pl.pallas_call(
        conv_kernel,
        out_shape=array(4, 1024, 128),
        in_specs=[VMEM] * 7,
        out_specs=VMEM,
        scratch_shapes=[
            pltpu.VMEM((GROUP * 64, 1536), BF16),
            pltpu.VMEM((OWN * 64, 512), F32),
            pltpu.VMEM((OWN * 64, 512), F32),
        ],
        compiler_params=pltpu.CompilerParams(vmem_limit_bytes=48 * 2**20),
        name="conv",
    )(filt, signal, *[jnp.asarray(table) for table in tables()])
    return pl.pallas_call(
        project_kernel,
        out_shape=array(512, 1024),
        in_specs=[VMEM] * 4 + [ANY],
        out_specs=VMEM,
        scratch_shapes=[
            pltpu.VMEM((1024, 4096), BF16),
            pltpu.VMEM((4, 1024, 128), F32),
            pltpu.VMEM((128, 1024), BF16),
            pltpu.VMEM((4, 128, 1024), F32),
            pltpu.VMEM((4, 2, 128, 1024), F32),
            pltpu.VMEM((4, 128, 1024), F32),
            pltpu.VMEM((4, 2, 128, 1024), F32),
            DMA((4,)),
            DMA((4,)),
            DMA((4, 2)),
            DMA((4, 2)),
            DMA((4, 2)),
            DMA((4, 2)),
            DMA,
        ],
        compiler_params=pltpu.CompilerParams(
            collective_id=1, has_side_effects=True, vmem_limit_bytes=48 * 2**20
        ),
        name="project",
    )(conv, gated, shortened_q, skip_gain[None], out_weight)


def solution(mesh):
    return jax.shard_map(
        per_device,
        mesh=mesh,
        in_specs=(
            P(None, "ctx", "tp"),
            P(None, None, "tp"),
            P("ctx", "tp"),
            P("tp"),
            P("tp", None),
        ),
        out_specs=P("ctx", "tp"),
        check_vma=False,
    )
```

time: 800 us -> 177 us (0.22); the launches traced: 790 us -> 175 us
  waiting for transfers between devices: 321 us -> 0 us
  matrix products: 235 us -> 0 us
  Pallas kernels: 0 us -> 170 us
  local copies, waits for them, and re-layouts: 97.1 us -> 4.78 us
  starting transfers between devices: 75.3 us -> 0 us
  blocking collectives: 36.5 us -> 0 us
  between operations: 14.4 us -> 0.08 us
  other arithmetic: 9.64 us -> 0 us
    dot_general x19 -> x0, matrix products: 235 us -> none  [the longest x18 229 us: exact_einsum(): return jnp.einsum(form, table, values, precision=lax.Precision.HIGHEST)]
    all_to_all x8 -> x0, waiting for transfers between devices: 224 us -> none  [the longest x1 43 us: per_device(): lax.all_to_all(signal_imag, 'ctx', split_axis=0, concat_axis=1, tiled=True)]
    pallas_call x0 -> x3, Pallas kernels: none -> 170 us  [the longest x1 89.8 us: per_device(): pl.pallas_call(project_kernel, out_shape=array(512, 1024), in_specs=[VMEM...]
    reduce_scatter x1 -> x0, waiting for transfers between devices: 80.3 us -> none  [per_device(): return lax.psum_scatter(terms, 'tp', scatter_dimension=1, tiled=True)]
    all_to_all x8 -> x0, starting transfers between devices: 73.2 us -> none  [the longest x1 11.8 us: per_device(): lax.all_to_all(gated[None], 'ctx', split_axis=1, concat_axis=0, tiled=True)]
    all_to_all x10 -> x0, local copies, waits for them, and re-layouts: 40 us -> none  [the longest x3 15.1 us: per_device(): lax.all_to_all(inverse_imaginary, 'ctx', split_axis=1, concat_axis=0, til...]
    all_to_all x1 -> x0, blocking collectives: 36.5 us -> none  [per_device(): lax.all_to_all(conv_blocks, 'ctx', split_axis=0, concat_axis=1, tiled=True)]
    sub x3 -> x0, local copies, waits for them, and re-layouts: 20.7 us -> none  [twist(): real_part * cosines - imag_part * sines]
  transfers between devices with their start and end apart: 10 -> 0, of which waited for: 8 -> 0; matrix products, arithmetic and copies ran while one was open for 20% -> 0% of each run, Pallas kernels for 0% -> 0%
where the time goes in v1:
time: 177 us; the launch traced here: 175 us
  Pallas kernels  170 us (96%)
  local copies, waits for them, and re-layouts  4.78 us (3%)
    pallas_call x1, Pallas kernels, per_device(): pl.pallas_call(project_kernel, out_shape=array(512, 1024), in_specs=[VMEM...  89.8 us
    pallas_call x1, Pallas kernels, per_device(): pl.pallas_call(spread_kernel, out_shape=(array(4, 1024, 128), array(4, 10...  59.4 us
    pallas_call x1, Pallas kernels, per_device(): pl.pallas_call(conv_kernel, out_shape=array(4, 1024, 128), in_specs=[VMEM...  20.7 us
    unnamed x19, local copies, waits for them, and re-layouts  4.78 us

profile of v1, /device:TPU:64, one launch (start us, length us, event | category | flops | bytes accessed | tf_op | source)
XLA Modules:
  0.0 174.8 jit_solution(14556643218496052050)
XLA Ops:
  0.0 0.0 copy-start.6
  0.0 0.8 copy-done.6
  0.8 0.0 copy-start.2
  0.8 0.0 copy-start.3
  0.8 0.0 copy-start.4
  0.8 0.0 copy-start.5
  0.8 0.0 copy-start.7
  0.8 59.4 %spread.1 = (f32[4,1024,128]{2,1,0:T(8,128)S(1)}, f32[4,1024,128]{2,1,0:T(8,128)S(1)}, f32[512,1024]{1,0:T(8,128)}, f32[512,1024]{1,0:T(8,128)}) custom-call(f32[3,512,1024]{2,1,0:T(8,128)} %projected.1, f32[3,3,1024]{2,1,0:T(4,128)S(1)} %copy-done.6, f32[512,1024]{1,0:T(8,128)} %long_filter.1), custom_call_target="tpu_custom_call" | custom-call | tf_op jit(solution)/shard_map/spread/pallas_call | solution.py:334
  60.2 0.0 copy-start
  60.2 1.3 copy-done
  61.5 0.0 copy-start.1
  61.5 1.3 copy-done.1
  62.9 0.0 copy-done.2
  62.9 0.0 copy-done.3
  62.9 0.0 copy-done.4
  62.9 0.0 copy-done.5
  62.9 0.0 copy-done.7
  62.9 0.0 copy-start.8
  62.9 20.7 %conv.1 = f32[4,1024,128]{2,1,0:T(8,128)S(1)} custom-call(f32[4,1024,128]{2,1,0:T(8,128)} %copy-done, f32[4,1024,128]{2,1,0:T(8,128)} %copy-done.1, bf16[128,192]{1,0:T(8,128)(2,1)S(1)} %copy-done.5, f32[2,64,256]{2,1,0:T(8,128)S(1)} %copy-done.4, bf16[1536,512]{1,0:T(8,128)(2,1)S(1)} %copy-done.3, bf16[1536,512]{1,0:T(8,128)(2,1)S(1)} %copy-done.2, ...), custom_call_target="tpu_custom_call" | custom-call | tf_op jit(solution)/shard_map/conv/pallas_call | solution.py:354
  83.6 0.0 copy-done.8
  83.6 89.8 %project.1 = f32[512,1024]{1,0:T(8,128)S(1)} custom-call(f32[4,1024,128]{2,1,0:T(8,128)S(1)} %conv.1, f32[512,1024]{1,0:T(8,128)} %get-tuple-element.11.gated, f32[512,1024]{1,0:T(8,128)} %get-tuple-element.12.shortened_q, f32[1,1024]{1,0:T(1,128)S(1)} %bitcast.1, bf16[1024,4096]{1,0:T(8,128)(2,1)} %weight_hbm.1), custom_call_target="tpu_custom_call" | custom-call | tf_op jit(solution)/shard_map/project/pallas_call | solution.py:367
  173.5 1.3 copy.12
Async XLA Ops:
  0.0 0.8 copy-start.6
  0.8 62.1 %copy-start.2 = (bf16[1536,512]{1,0:T(8,128)(2,1)S(1)}, bf16[1536,512]{1,0:T(8,128)(2,1)}, u32[]{:S(2)}) copy-start(bf16[1536,512]{1,0:T(8,128)(2,1)} %constant.13.clone.back_second) | copy-start | bytes 4718596
  0.8 62.1 %copy-start.3 = (bf16[1536,512]{1,0:T(8,128)(2,1)S(1)}, bf16[1536,512]{1,0:T(8,128)(2,1)}, u32[]{:S(2)}) copy-start(bf16[1536,512]{1,0:T(8,128)(2,1)} %constant.12.clone.second) | copy-start | bytes 4718596
  0.8 62.1 %copy-start.4 = (f32[2,64,256]{2,1,0:T(8,128)S(1)}, f32[2,64,256]{2,1,0:T(8,128)}, u32[]{:S(2)}) copy-start(f32[2,64,256]{2,1,0:T(8,128)} %constant.11.clone.twist) | copy-start | bytes 393220
  0.8 62.1 %copy-start.5 = (bf16[128,192]{1,0:T(8,128)(2,1)S(1)}, bf16[128,192]{1,0:T(8,128)(2,1)}, u32[]{:S(2)}) copy-start(bf16[128,192]{1,0:T(8,128)(2,1)} %constant.10.clone.first) | copy-start | bytes 147460
  0.8 62.1 %copy-start.7 = (bf16[64,384]{1,0:T(8,128)(2,1)S(1)}, bf16[64,384]{1,0:T(8,128)(2,1)}, u32[]{:S(2)}) copy-start(bf16[64,384]{1,0:T(8,128)(2,1)} %constant.14.clone.back_first) | copy-start | bytes 147460
  60.2 1.3 copy-start
  61.5 1.3 copy-start.1
  62.9 20.7 %copy-start.8 = (f32[1024]{0:T(1024)S(1)}, f32[1024]{0:T(1024)}, u32[]{:S(2)}) copy-start(f32[1024]{0:T(1024)} %param.13) | copy-start | bytes 12292

commit v2 on v1

v2 whole, which is shorter than its diff:
```python
import jax
import jax.numpy as jnp
import ml_dtypes
import numpy as np
from jax import lax
from jax.experimental import pallas as pl
from jax.experimental.pallas import tpu as pltpu
from jax.sharding import PartitionSpec as P

MESH = pl.DeviceIdType.MESH
BF16 = jnp.bfloat16
F32 = jnp.float32
CTX = 32
TP = 4
OWN = 32
GROUP = 8
GROUPS = OWN // GROUP
CHIP_OFFSETS = (
    (1, 0), (3, 0), (0, 1), (0, 3), (1, 1), (3, 3), (1, 3), (3, 1),
    (2, 0), (0, 2), (2, 1), (2, 3), (1, 2), (3, 2), (2, 2),
)
PEERS = tuple((a, b, d) for a, b in CHIP_OFFSETS for d in (0, 1)) + ((0, 0, 1),)


def split_np(table):
    high = table.astype(ml_dtypes.bfloat16)
    low = (table - high.astype(np.float64)).astype(ml_dtypes.bfloat16)
    return high, low


def tables():
    block = np.arange(32)
    n1 = np.concatenate([2 * block, 2 * block + 1]).astype(np.float64)
    k1 = np.arange(64) + 0.25
    n2 = np.arange(256)
    psi = 2 * np.pi * np.outer(k1, n1) / 64
    high, low = split_np(np.concatenate([np.cos(psi), -np.sin(psi)], 0))
    first = np.concatenate([high, high, low], 1)
    phi = 2 * np.pi * np.outer(k1, n2) / 16384
    twist = np.stack([np.cos(phi), np.sin(phi)]).astype(np.float32)
    theta = 2 * np.pi * (np.outer(n2, n2) % 256) / 256
    cosine, sine = np.cos(theta), np.sin(theta)
    high, low = split_np(np.block([[cosine, -sine], [sine, cosine]]))
    second = np.concatenate([high, high, low], 0)
    high, low = split_np(np.block([[cosine, sine], [-sine, cosine]]))
    back_second = np.concatenate([high, high, low], 0)
    high, low = split_np(np.concatenate([np.cos(psi.T), -np.sin(psi.T)], 1) / 16384)
    back_first = np.concatenate([high, high, low], 1)
    return first, twist, second, back_second, back_first


def split(value):
    high = value.astype(BF16)
    return high, (value - high.astype(F32)).astype(BF16)


def dot(left, right):
    return jnp.dot(left, right, preferred_element_type=F32)


def ctx_peer(me, offset):
    a, b, d = offset
    return (me // 8 + a) % 4 * 8 + (me // 2 + b) % 4 * 2 + (me + d) % 2


def rows_of(device):
    return pl.ds(pl.multiple_of(device * OWN, OWN), OWN)


def send_slabs(source, target, slab, own_slab, me, tp, send_sem, recv_sem):
    pltpu.make_async_copy(
        source.at[:, slab(me), :], target.at[:, own_slab, :], recv_sem
    ).start()
    for offset in PEERS:
        peer = ctx_peer(me, offset)
        pltpu.make_async_remote_copy(
            src_ref=source.at[:, slab(peer), :],
            dst_ref=target.at[:, own_slab, :],
            send_sem=send_sem,
            recv_sem=recv_sem,
            device_id=(peer, tp),
            device_id_type=MESH,
        ).start()


def wait_arrived(target, recv_sem):
    pltpu.make_async_copy(target, target, recv_sem).wait()


def wait_sent(source, send_sem):
    away = source.at[:, 0 : (CTX - 1) * OWN, :]
    pltpu.make_async_copy(away, away, send_sem).wait()


def short_conv(projected, halo, short_filters, stream, jb, cols):
    rows = projected[stream, jb * 128 : jb * 128 + 128, cols]
    before = halo[stream, :, cols] if jb == 0 else projected[stream, jb * 128 - 8 : jb * 128, cols]
    longer = jnp.concatenate([before, rows], 0)
    taps = short_filters[stream, :, cols]
    return taps[0:1] * rows + taps[1:2] * longer[7:135] + taps[2:3] * longer[6:134]


def mixer_kernel(
    projected_hbm, short_filters, long_filter_hbm, skip_gain, weight_hbm,
    first, twist, second, back_second, back_first,
    out,
    projected, long_filter, weight, halo, halo_in, filt_t, gated_t, filt, signal,
    gated, shortened_q, rows, spectrum, conv_in, gated_out, far, near, far_in, near_in,
    load_sem, halo_send, halo_recv, filt_send, filt_recv, signal_send, signal_recv,
    conv_send, conv_recv, far_send, far_recv, near_send, near_recv,
):
    me = lax.axis_index("ctx")
    tp = lax.axis_index("tp")
    up, down = lax.rem(tp + 1, TP), lax.rem(tp + TP - 1, TP)
    conv = filt_t

    barrier = pltpu.get_barrier_semaphore()

    def signal_peer(i, carry):
        pl.semaphore_signal(
            barrier, inc=1, device_id=(lax.rem(me + i, CTX), tp), device_id_type=MESH
        )
        return carry

    lax.fori_loop(1, CTX, signal_peer, 0)
    for side in (up, down):
        pl.semaphore_signal(barrier, inc=1, device_id=(me, side), device_id_type=MESH)
    load_filter = pltpu.make_async_copy(long_filter_hbm, long_filter, load_sem.at[0])
    load_filter.start()
    load_projected = pltpu.make_async_copy(projected_hbm, projected, load_sem.at[1])
    load_projected.start()
    load_weight = pltpu.make_async_copy(weight_hbm, weight, load_sem.at[2])
    load_weight.start()
    load_filter.wait()

    def turn_filter(cb, carry):
        cols = pl.ds(pl.multiple_of(cb * 128, 128), 128)
        for jb in range(4):
            filt_t[jb, cols, :] = long_filter[jb * 128 : jb * 128 + 128, cols].T
        return carry

    lax.fori_loop(0, 8, turn_filter, 0)
    pl.semaphore_wait(barrier, CTX + 1)

    edge = pltpu.make_async_remote_copy(
        src_ref=projected_hbm.at[:, 504:512, :],
        dst_ref=halo_in,
        send_sem=halo_send,
        recv_sem=halo_recv,
        device_id=(lax.rem(me + 1, CTX), tp),
        device_id_type=MESH,
    )
    edge.start()
    for half in range(2):
        part = pl.ds(2 * half, 2)
        send_slabs(
            filt_t.at[part], filt.at[part], rows_of, rows_of(me), me, tp, filt_send, filt_recv
        )
    load_projected.wait()
    edge.wait()
    halo[...] = jnp.where(me > 0, halo_in[...], 0.0)

    def gate(cb, carry):
        cols = pl.ds(pl.multiple_of(cb * 128, 128), 128)
        for jb in range(4):
            key = short_conv(projected, halo, short_filters, 1, jb, cols)
            value = short_conv(projected, halo, short_filters, 2, jb, cols)
            product = key * value
            gated[jb * 128 : jb * 128 + 128, cols] = product
            gated_t[jb, cols, :] = product.T
        return carry

    lax.fori_loop(0, 8, gate, 0)

    def send_group(group, carry):
        def slab(device):
            return pl.ds(pl.multiple_of(device * OWN + group * GROUP, GROUP), GROUP)

        send_slabs(
            gated_t, signal.at[group], slab, pl.ds(pl.multiple_of(me * GROUP, GROUP), GROUP),
            me, tp, signal_send, signal_recv.at[group],
        )
        return carry

    lax.fori_loop(0, GROUPS, send_group, 0)

    def query(cb, carry):
        cols = pl.ds(pl.multiple_of(cb * 128, 128), 128)
        for jb in range(4):
            shortened_q[jb * 128 : jb * 128 + 128, cols] = short_conv(
                projected, halo, short_filters, 0, jb, cols
            )
        return carry

    lax.fori_loop(0, 8, query, 0)

    cosine, sine = twist[0], twist[1]

    def forward(load_block):
        for i in range(GROUP):
            blocks = [load_block(i, jb) for jb in range(4)]
            high, low = split(
                jnp.concatenate(
                    [jnp.concatenate(blocks[:2], 1), jnp.concatenate(blocks[2:], 1)], 0
                )
            )
            turned = dot(first[...], jnp.concatenate([high, low, high], 0))
            real, imag = turned[:64], turned[64:]
            real_high, real_low = split(real * cosine + imag * sine)
            imag_high, imag_low = split(imag * cosine - real * sine)
            rows[i * 64 : i * 64 + 64, :] = jnp.concatenate(
                [real_high, imag_high, real_low, imag_low, real_high, imag_high], 1
            )
        return dot(rows[...], second[...])

    def group_rows(group):
        return pl.ds(pl.multiple_of(group * GROUP * 64, GROUP * 64), GROUP * 64)

    def filter_step(group, carry):
        spectrum[group_rows(group), :] = forward(
            lambda i, jb: filt[jb, pl.ds(group * GROUP + i, CTX, stride=OWN), :]
        )
        return carry

    wait_arrived(filt, filt_recv)
    lax.fori_loop(0, GROUPS, filter_step, 0)

    def signal_step(group, carry):
        wait_arrived(signal.at[group], signal_recv.at[group])
        left = forward(lambda i, jb: signal[group, jb, pl.ds(i, CTX, stride=GROUP), :])
        right = spectrum[group_rows(group), :]
        left_real, left_imag = left[:, :256], left[:, 256:]
        right_real, right_imag = right[:, :256], right[:, 256:]
        real_high, real_low = split(left_real * right_real - left_imag * right_imag)
        imag_high, imag_low = split(left_real * right_imag + left_imag * right_real)
        product = jnp.concatenate(
            [real_high, imag_high, real_low, imag_low, real_high, imag_high], 1
        )
        spectrum[group_rows(group), :] = dot(product, back_second[...])
        return carry

    lax.fori_loop(0, GROUPS, signal_step, 0)
    wait_sent(filt_t, filt_send)

    def back(half):
        lanes = slice(128 * half, 128 * half + 128)
        imag_lanes = slice(256 + 128 * half, 384 + 128 * half)
        cosine, sine = twist[0, :, lanes], twist[1, :, lanes]

        def step(group, carry):
            for i in range(GROUP):
                channel = group * GROUP + i
                block = pl.ds(pl.multiple_of(channel * 64, 64), 64)
                real, imag = spectrum[block, lanes], spectrum[block, imag_lanes]
                real_high, real_low = split(real * cosine - imag * sine)
                imag_high, imag_low = split(imag * cosine + real * sine)
                result = dot(
                    back_first[...],
                    jnp.concatenate(
                        [real_high, imag_high, real_low, imag_low, real_high, imag_high], 0
                    ),
                )
                conv[half, pl.ds(channel, CTX, stride=OWN), :] = result[:32]
                conv[half + 2, pl.ds(channel, CTX, stride=OWN), :] = result[32:]
            return carry

        lax.fori_loop(0, GROUPS, step, 0)
        for jb in (half, half + 2):
            chunk = pl.ds(jb, 1)
            send_slabs(
                conv.at[chunk], conv_in.at[chunk], rows_of, rows_of(me),
                me, tp, conv_send.at[jb], conv_recv.at[jb],
            )

    back(0)
    back(1)
    load_weight.wait()

    def columns(quarter):
        return pl.ds(pl.multiple_of(quarter * 1024, 1024), 1024)

    def to_far(jb, side):
        half = slice(512 * side, 512 * side + 512)
        return pltpu.make_async_remote_copy(
            src_ref=far.at[jb, :, half],
            dst_ref=far_in.at[jb, :, half],
            send_sem=far_send.at[jb, side],
            recv_sem=far_recv.at[jb, side],
            device_id=(me, (up, down)[side]),
            device_id_type=MESH,
        )

    def to_near(jb, side):
        return pltpu.make_async_remote_copy(
            src_ref=near.at[jb, side],
            dst_ref=near_in.at[jb, side],
            send_sem=near_send.at[jb, side],
            recv_sem=near_recv.at[jb, side],
            device_id=(me, (up, down)[side]),
            device_id_type=MESH,
        )

    def compute(jb):
        wait_arrived(conv_in.at[pl.ds(jb, 1)], conv_recv.at[jb])
        tokens = slice(jb * 128, jb * 128 + 128)
        mixed = conv_in[jb].T + skip_gain[...] * gated[tokens, :]
        gated_out[...] = (shortened_q[tokens, :] * mixed).astype(BF16)
        far[jb] = dot(gated_out[...], weight[:, columns(lax.rem(tp + 2, TP))])
        to_far(jb, 0).start()
        to_far(jb, 1).start()
        near[jb, 0] = dot(gated_out[...], weight[:, columns(up)])
        near[jb, 1] = dot(gated_out[...], weight[:, columns(down)])
        out[tokens, :] = dot(gated_out[...], weight[:, columns(tp)])

    def relay(jb):
        for side in (0, 1):
            half = slice(512 * side, 512 * side + 512)
            to_far(jb, side).wait_recv()
            near[jb, side, :, half] += far_in[jb, :, half]
            to_near(jb, side).start()

    order = (0, 2, 1, 3)
    compute(order[0])
    for step in range(1, 4):
        compute(order[step])
        relay(order[step - 1])
    relay(order[3])
    for jb in order:
        tokens = slice(jb * 128, jb * 128 + 128)
        to_near(jb, 0).wait_recv()
        to_near(jb, 1).wait_recv()
        out[tokens, :] += near_in[jb, 0] + near_in[jb, 1]
    wait_sent(gated_t, signal_send)
    for jb in range(4):
        wait_sent(conv.at[pl.ds(jb, 1)], conv_send.at[jb])
        for side in (0, 1):
            to_far(jb, side).wait_send()
            to_near(jb, side).wait_send()


VMEM = pl.BlockSpec(memory_space=pltpu.VMEM)
ANY = pl.BlockSpec(memory_space=pl.ANY)
DMA = pltpu.SemaphoreType.DMA


def per_device(projected, short_filters, long_filter, skip_gain, out_weight):
    return pl.pallas_call(
        mixer_kernel,
        out_shape=jax.ShapeDtypeStruct((512, 1024), F32),
        in_specs=[ANY, VMEM, ANY, VMEM, ANY] + [VMEM] * 5,
        out_specs=VMEM,
        scratch_shapes=[
            pltpu.VMEM((3, 512, 1024), F32),
            pltpu.VMEM((512, 1024), F32),
            pltpu.VMEM((1024, 4096), BF16),
            pltpu.VMEM((3, 8, 1024), F32),
            pltpu.VMEM((3, 8, 1024), F32),
            pltpu.VMEM((4, 1024, 128), F32),
            pltpu.VMEM((4, 1024, 128), F32),
            pltpu.VMEM((4, 1024, 128), F32),
            pltpu.VMEM((GROUPS, 4, CTX * GROUP, 128), F32),
            pltpu.VMEM((512, 1024), F32),
            pltpu.VMEM((512, 1024), F32),
            pltpu.VMEM((GROUP * 64, 1536), BF16),
            pltpu.VMEM((OWN * 64, 512), F32),
            pltpu.VMEM((4, 1024, 128), F32),
            pltpu.VMEM((128, 1024), BF16),
            pltpu.VMEM((4, 128, 1024), F32),
            pltpu.VMEM((4, 2, 128, 1024), F32),
            pltpu.VMEM((4, 128, 1024), F32),
            pltpu.VMEM((4, 2, 128, 1024), F32),
            DMA((3,)),
            DMA,
            DMA,
            DMA,
            DMA,
            DMA,
            DMA((GROUPS,)),
            DMA((4,)),
            DMA((4,)),
            DMA((4, 2)),
            DMA((4, 2)),
            DMA((4, 2)),
            DMA((4, 2)),
        ],
        compiler_params=pltpu.CompilerParams(
            collective_id=0, has_side_effects=True, vmem_limit_bytes=60 * 2**20
        ),
        name="mixer",
    )(
        projected, short_filters, long_filter, skip_gain[None], out_weight,
        *[jnp.asarray(table) for table in tables()],
    )


def solution(mesh):
    return jax.shard_map(
        per_device,
        mesh=mesh,
        in_specs=(
            P(None, "ctx", "tp"),
            P(None, None, "tp"),
            P("ctx", "tp"),
            P("tp"),
            P("tp", None),
        ),
        out_specs=P("ctx", "tp"),
        check_vma=False,
    )
```

time: 177 us -> 149 us (0.84)
  Pallas kernels: 170 us -> 144 us
    pallas_call x3 -> x1, Pallas kernels: 170 us -> 144 us  [per_device(): pl.pallas_call(mixer_kernel, out_shape=jax.ShapeDtypeStruct((512, 1024),...]
    unnamed x19 -> x1, local copies, waits for them, and re-layouts: 4.78 us -> 3.16 us
where the time goes in v2:
time: 149 us; the launch traced here: 147 us
  Pallas kernels  144 us (97%)
  local copies, waits for them, and re-layouts  3.16 us (2%)
    pallas_call x1, Pallas kernels, per_device(): pl.pallas_call(mixer_kernel, out_shape=jax.ShapeDtypeStruct((512, 1024),...  144 us
    unnamed x1, local copies, waits for them, and re-layouts  3.16 us

profile of v2, /device:TPU:64, one launch (start us, length us, event | category | flops | bytes accessed | tf_op | source)
XLA Modules:
  0.0 146.7 jit_solution(10467726366397823036)
XLA Ops:
  0.0 143.6 %mixer.1 = f32[512,1024]{1,0:T(8,128)} custom-call(f32[3,512,1024]{2,1,0:T(8,128)} %projected_hbm.1, f32[3,3,1024]{2,1,0:T(4,128)} %short_filters.1, f32[512,1024]{1,0:T(8,128)} %long_filter_hbm.1, f32[1,1024]{1,0:T(1,128)} %bitcast.1, bf16[1024,4096]{1,0:T(8,128)(2,1)} %weight_hbm.1, bf16[128,192]{1,0:T(8,128)(2,1)} %constant.10.clone.first, ...), custom_call_target="tpu_custom_call" | custom-call | tf_op jit(solution)/shard_map/mixer/pallas_call | solution.py:347
  143.6 3.2 %copy.12 = f32[512,1024]{1,0:T(8,128)} copy(f32[512,1024]{1,0:T(8,128)} %mixer.1) | data formatting | bytes 4194304

commit v3 on v2

--- a/solution.py
+++ b/solution.py
@@ -102,10 +102,11 @@
 
 def mixer_kernel(
     projected_hbm, short_filters, long_filter_hbm, skip_gain, weight_hbm,
-    first, twist, second, back_second, back_first,
+    first_hbm, twist_hbm, second_hbm, back_second_hbm, back_first_hbm,
     out,
-    projected, long_filter, weight, halo, halo_in, filt_t, gated_t, filt, signal,
-    gated, shortened_q, rows, spectrum, conv_in, gated_out, far, near, far_in, near_in,
+    projected, long_filter, weight, first, twist, second, back_second, back_first,
+    halo, halo_in, filt_t, gated_t, filt, signal,
+    shortened_q, rows, spectrum, conv_in, gated_out, far_in, near_in,
     load_sem, halo_send, halo_recv, filt_send, filt_recv, signal_send, signal_recv,
     conv_send, conv_recv, far_send, far_recv, near_send, near_recv,
 ):
@@ -113,6 +114,13 @@
     tp = lax.axis_index("tp")
     up, down = lax.rem(tp + 1, TP), lax.rem(tp + TP - 1, TP)
     conv = filt_t
+    gated = long_filter
+
+    def far(jb):
+        return projected.at[0, pl.ds(jb * 128, 128), :]
+
+    def near(jb, side):
+        return projected.at[1 + side, pl.ds(jb * 128, 128), :]
 
     barrier = pltpu.get_barrier_semaphore()
 
@@ -129,8 +137,6 @@
     load_filter.start()
     load_projected = pltpu.make_async_copy(projected_hbm, projected, load_sem.at[1])
     load_projected.start()
-    load_weight = pltpu.make_async_copy(weight_hbm, weight, load_sem.at[2])
-    load_weight.start()
     load_filter.wait()
 
     def turn_filter(cb, carry):
@@ -157,6 +163,19 @@
             filt_t.at[part], filt.at[part], rows_of, rows_of(me), me, tp, filt_send, filt_recv
         )
     load_projected.wait()
+    load_tables = [
+        pltpu.make_async_copy(source, target, load_sem.at[3 + i])
+        for i, (source, target) in enumerate(
+            (
+                (first_hbm, first), (twist_hbm, twist), (second_hbm, second),
+                (back_second_hbm, back_second), (back_first_hbm, back_first),
+            )
+        )
+    ]
+    for load in load_tables:
+        load.start()
+    load_weight = pltpu.make_async_copy(weight_hbm, weight, load_sem.at[2])
+    load_weight.start()
     edge.wait()
     halo[...] = jnp.where(me > 0, halo_in[...], 0.0)
 
@@ -194,6 +213,8 @@
 
     lax.fori_loop(0, 8, query, 0)
 
+    for load in load_tables:
+        load.wait()
     cosine, sine = twist[0], twist[1]
 
     def forward(load_block):
@@ -237,34 +258,33 @@
             [real_high, imag_high, real_low, imag_low, real_high, imag_high], 1
         )
         spectrum[group_rows(group), :] = dot(product, back_second[...])
-        return carry
-
-    lax.fori_loop(0, GROUPS, signal_step, 0)
-    wait_sent(filt_t, filt_send)
-
-    def back(half):
+        back(0, group)
+        return carry
+
+    def back(half, group):
         lanes = slice(128 * half, 128 * half + 128)
         imag_lanes = slice(256 + 128 * half, 384 + 128 * half)
         cosine, sine = twist[0, :, lanes], twist[1, :, lanes]
-
-        def step(group, carry):
-            for i in range(GROUP):
-                channel = group * GROUP + i
-                block = pl.ds(pl.multiple_of(channel * 64, 64), 64)
-                real, imag = spectrum[block, lanes], spectrum[block, imag_lanes]
-                real_high, real_low = split(real * cosine - imag * sine)
-                imag_high, imag_low = split(imag * cosine + real * sine)
-                result = dot(
-                    back_first[...],
-                    jnp.concatenate(
-                        [real_high, imag_high, real_low, imag_low, real_high, imag_high], 0
-                    ),
-                )
-                conv[half, pl.ds(channel, CTX, stride=OWN), :] = result[:32]
-                conv[half + 2, pl.ds(channel, CTX, stride=OWN), :] = result[32:]
-            return carry
-
-        lax.fori_loop(0, GROUPS, step, 0)
+        for i in range(GROUP):
+            channel = group * GROUP + i
+            block = pl.ds(pl.multiple_of(channel * 64, 64), 64)
+            real, imag = spectrum[block, lanes], spectrum[block, imag_lanes]
+            real_high, real_low = split(real * cosine - imag * sine)
+            imag_high, imag_low = split(imag * cosine + real * sine)
+            result = dot(
+                back_first[...],
+                jnp.concatenate(
+                    [real_high, imag_high, real_low, imag_low, real_high, imag_high], 0
+                ),
+            )
+            conv[half, pl.ds(channel, CTX, stride=OWN), :] = result[:32]
+            conv[half + 2, pl.ds(channel, CTX, stride=OWN), :] = result[32:]
+
+    def back_step(group, carry):
+        back(1, group)
+        return carry
+
+    def return_half(half):
         for jb in (half, half + 2):
             chunk = pl.ds(jb, 1)
             send_slabs(
@@ -272,8 +292,11 @@
                 me, tp, conv_send.at[jb], conv_recv.at[jb],
             )
 
-    back(0)
-    back(1)
+    wait_sent(filt_t, filt_send)
+    lax.fori_loop(0, GROUPS, signal_step, 0)
+    return_half(0)
+    lax.fori_loop(0, GROUPS, back_step, 0)
+    return_half(1)
     load_weight.wait()
 
     def columns(quarter):
@@ -282,7 +305,7 @@
     def to_far(jb, side):
         half = slice(512 * side, 512 * side + 512)
         return pltpu.make_async_remote_copy(
-            src_ref=far.at[jb, :, half],
+            src_ref=far(jb).at[:, half],
             dst_ref=far_in.at[jb, :, half],
             send_sem=far_send.at[jb, side],
             recv_sem=far_recv.at[jb, side],
@@ -292,7 +315,7 @@
 
     def to_near(jb, side):
         return pltpu.make_async_remote_copy(
-            src_ref=near.at[jb, side],
+            src_ref=near(jb, side),
             dst_ref=near_in.at[jb, side],
             send_sem=near_send.at[jb, side],
             recv_sem=near_recv.at[jb, side],
@@ -305,18 +328,18 @@
         tokens = slice(jb * 128, jb * 128 + 128)
         mixed = conv_in[jb].T + skip_gain[...] * gated[tokens, :]
         gated_out[...] = (shortened_q[tokens, :] * mixed).astype(BF16)
-        far[jb] = dot(gated_out[...], weight[:, columns(lax.rem(tp + 2, TP))])
+        far(jb)[...] = dot(gated_out[...], weight[:, columns(lax.rem(tp + 2, TP))])
         to_far(jb, 0).start()
         to_far(jb, 1).start()
-        near[jb, 0] = dot(gated_out[...], weight[:, columns(up)])
-        near[jb, 1] = dot(gated_out[...], weight[:, columns(down)])
+        near(jb, 0)[...] = dot(gated_out[...], weight[:, columns(up)])
+        near(jb, 1)[...] = dot(gated_out[...], weight[:, columns(down)])
         out[tokens, :] = dot(gated_out[...], weight[:, columns(tp)])
 
     def relay(jb):
         for side in (0, 1):
             half = slice(512 * side, 512 * side + 512)
             to_far(jb, side).wait_recv()
-            near[jb, side, :, half] += far_in[jb, :, half]
+            near(jb, side)[:, half] += far_in[jb, :, half]
             to_near(jb, side).start()
 
     order = (0, 2, 1, 3)
@@ -339,7 +362,7 @@
 
 
 VMEM = pl.BlockSpec(memory_space=pltpu.VMEM)
-ANY = pl.BlockSpec(memory_space=pl.ANY)
+HBM = pl.BlockSpec(memory_space=pltpu.HBM)
 DMA = pltpu.SemaphoreType.DMA
 
 
@@ -347,12 +370,17 @@
     return pl.pallas_call(
         mixer_kernel,
         out_shape=jax.ShapeDtypeStruct((512, 1024), F32),
-        in_specs=[ANY, VMEM, ANY, VMEM, ANY] + [VMEM] * 5,
+        in_specs=[HBM, VMEM, HBM, VMEM, HBM] + [HBM] * 5,
         out_specs=VMEM,
         scratch_shapes=[
             pltpu.VMEM((3, 512, 1024), F32),
             pltpu.VMEM((512, 1024), F32),
             pltpu.VMEM((1024, 4096), BF16),
+            pltpu.VMEM((128, 192), BF16),
+            pltpu.VMEM((2, 64, 256), F32),
+            pltpu.VMEM((1536, 512), BF16),
+            pltpu.VMEM((1536, 512), BF16),
+            pltpu.VMEM((64, 384), BF16),
             pltpu.VMEM((3, 8, 1024), F32),
             pltpu.VMEM((3, 8, 1024), F32),
             pltpu.VMEM((4, 1024, 128), F32),
@@ -360,16 +388,13 @@
             pltpu.VMEM((4, 1024, 128), F32),
             pltpu.VMEM((GROUPS, 4, CTX * GROUP, 128), F32),
             pltpu.VMEM((512, 1024), F32),
-            pltpu.VMEM((512, 1024), F32),
             pltpu.VMEM((GROUP * 64, 1536), BF16),
             pltpu.VMEM((OWN * 64, 512), F32),
             pltpu.VMEM((4, 1024, 128), F32),
             pltpu.VMEM((128, 1024), BF16),
             pltpu.VMEM((4, 128, 1024), F32),
             pltpu.VMEM((4, 2, 128, 1024), F32),
-            pltpu.VMEM((4, 128, 1024), F32),
-            pltpu.VMEM((4, 2, 128, 1024), F32),
-            DMA((3,)),
+            DMA((8,)),
             DMA,
             DMA,
             DMA,

time: 149 us -> 147 us (0.987)
  Pallas kernels: 144 us -> 141 us
    pallas_call x1, Pallas kernels: 144 us -> 141 us  [per_device(): pl.pallas_call(mixer_kernel, out_shape=jax.ShapeDtypeStruct((512, 1024),...]
where the time goes in v3:
time: 147 us; the launch traced here: 144 us
  Pallas kernels  141 us (96%)
  local copies, waits for them, and re-layouts  3.16 us (2%)
    pallas_call x1, Pallas kernels, per_device(): pl.pallas_call(mixer_kernel, out_shape=jax.ShapeDtypeStruct((512, 1024),...  141 us
    unnamed x1, local copies, waits for them, and re-layouts  3.16 us

profile of v3, /device:TPU:64, one launch (start us, length us, event | category | flops | bytes accessed | tf_op | source)
XLA Modules:
  0.0 144.2 jit_solution(12277658807442129334)
XLA Ops:
  0.0 141.1 %mixer.1 = f32[512,1024]{1,0:T(8,128)} custom-call(f32[3,512,1024]{2,1,0:T(8,128)} %projected_hbm.1, f32[3,3,1024]{2,1,0:T(4,128)} %short_filters.1, f32[512,1024]{1,0:T(8,128)} %long_filter_hbm.1, f32[1,1024]{1,0:T(1,128)} %bitcast.1, bf16[1024,4096]{1,0:T(8,128)(2,1)} %weight_hbm.1, bf16[128,192]{1,0:T(8,128)(2,1)} %constant.10.clone.first_hbm, ...), custom_call_target="tpu_custom_call" | custom-call | tf_op jit(solution)/shard_map/mixer/pallas_call | solution.py:370
  141.1 3.2 %copy.12 = f32[512,1024]{1,0:T(8,128)} copy(f32[512,1024]{1,0:T(8,128)} %mixer.1) | data formatting | bytes 4194304

commit v4 on v3

--- a/solution.py
+++ b/solution.py
@@ -106,21 +106,90 @@
     out,
     projected, long_filter, weight, first, twist, second, back_second, back_first,
     halo, halo_in, filt_t, gated_t, filt, signal,
-    shortened_q, rows, spectrum, conv_in, gated_out, far_in, near_in,
+    shortened_q, rows, spectrum, conv_in, gated_out, partner_out, weight_in, partner_weight,
+    gather_in, sum_in, near_in_partner,
     load_sem, halo_send, halo_recv, filt_send, filt_recv, signal_send, signal_recv,
-    conv_send, conv_recv, far_send, far_recv, near_send, near_recv,
+    conv_send, conv_recv, fetch_send, fetch_recv, share_send, share_recv, swap_send, swap_recv,
+    gather_send, gather_recv, sum_send, sum_recv, far_send, far_recv, near_send, near_recv,
 ):
     me = lax.axis_index("ctx")
     tp = lax.axis_index("tp")
-    up, down = lax.rem(tp + 1, TP), lax.rem(tp + TP - 1, TP)
+    partner, mate = tp + 1 - 2 * (tp % 2), TP - 1 - tp
+    parity = (me // 8 + me // 2) % 2
+    mine, theirs = 2 * parity + me % 2, 2 * (1 - parity) + me % 2
     conv = filt_t
     gated = long_filter
-
-    def far(jb):
+    fetch_out = out
+
+    def sum_out(jb):
         return projected.at[0, pl.ds(jb * 128, 128), :]
 
-    def near(jb, side):
-        return projected.at[1 + side, pl.ds(jb * 128, 128), :]
+    def gather_out(jb):
+        return projected.at[1, pl.ds(jb * 128, 128), :]
+
+    far = projected.at[0, pl.ds(0, 128), :]
+    near = (projected.at[1, pl.ds(0, 128), :], projected.at[2, pl.ds(0, 128), :])
+    far_in, near_in = gather_in.at[0], (sum_in.at[0], near_in_partner)
+
+    def columns(quarter):
+        return pl.ds(pl.multiple_of(quarter * 1024, 1024), 1024)
+
+    def quarter_rows(quarter):
+        return pl.ds(pl.multiple_of(quarter * 256, 256), 256)
+
+    def to_tp(source, target, device, send_sem, recv_sem):
+        return pltpu.make_async_remote_copy(
+            src_ref=source,
+            dst_ref=target,
+            send_sem=send_sem,
+            recv_sem=recv_sem,
+            device_id=(me, device),
+            device_id_type=MESH,
+        )
+
+    def fetch(part):
+        return to_tp(
+            fetch_out.at[pl.ds(part * 256, 256), :],
+            weight_in.at[quarter_rows(mine), pl.ds(part * 1024, 1024)],
+            partner, fetch_send.at[part], fetch_recv.at[part],
+        )
+
+    def share(part):
+        for direction, offset in enumerate(((1, 0, 0), (3, 0, 0), (0, 1, 0), (0, 3, 0))):
+            first_row = mine * 256 + direction * 64 + part * 32
+            slab = weight_in.at[pl.ds(pl.multiple_of(first_row, 32), 32), :]
+            pltpu.make_async_remote_copy(
+                src_ref=slab,
+                dst_ref=slab,
+                send_sem=share_send.at[part],
+                recv_sem=share_recv.at[part],
+                device_id=(ctx_peer(me, offset), tp),
+                device_id_type=MESH,
+            ).start()
+
+    def share_bytes():
+        return weight_in.at[pl.ds(pl.multiple_of(theirs * 256, 256), 128), :]
+
+    def swap(which):
+        slab = weight_in.at[quarter_rows((mine, theirs)[which]), :]
+        return pltpu.make_async_remote_copy(
+            src_ref=slab,
+            dst_ref=slab,
+            send_sem=swap_send.at[which],
+            recv_sem=swap_recv.at[which],
+            device_id=(ctx_peer(me, (0, 0, 1)), tp),
+            device_id_type=MESH,
+        )
+
+    def round_quarters(which):
+        first_row = ((parity, 1 - parity)[which]) * 512
+
+        def step(i, carry):
+            block = pl.ds(pl.multiple_of(first_row + i * 64, 64), 64)
+            partner_weight[block, :] = weight_in[block, :].astype(BF16)
+            return carry
+
+        lax.fori_loop(0, 8, step, 0)
 
     barrier = pltpu.get_barrier_semaphore()
 
@@ -131,12 +200,21 @@
         return carry
 
     lax.fori_loop(1, CTX, signal_peer, 0)
-    for side in (up, down):
+    for side in (partner, mate):
         pl.semaphore_signal(barrier, inc=1, device_id=(me, side), device_id_type=MESH)
     load_filter = pltpu.make_async_copy(long_filter_hbm, long_filter, load_sem.at[0])
     load_filter.start()
     load_projected = pltpu.make_async_copy(projected_hbm, projected, load_sem.at[1])
     load_projected.start()
+    load_weight = [
+        pltpu.make_async_copy(
+            weight_hbm.at[quarter_rows(lax.rem(mine + i, 4)), :],
+            weight.at[quarter_rows(lax.rem(mine + i, 4)), :],
+            load_sem.at[8 + i],
+        )
+        for i in range(4)
+    ]
+    load_weight[0].start()
     load_filter.wait()
 
     def turn_filter(cb, carry):
@@ -146,6 +224,11 @@
         return carry
 
     lax.fori_loop(0, 8, turn_filter, 0)
+    load_weight[0].wait()
+    for part, quarter in enumerate((partner, TP - 1 - partner)):
+        fetch_out[part * 256 : part * 256 + 256, :] = weight[
+            quarter_rows(mine), columns(quarter)
+        ].astype(F32)
     pl.semaphore_wait(barrier, CTX + 1)
 
     edge = pltpu.make_async_remote_copy(
@@ -162,6 +245,8 @@
         send_slabs(
             filt_t.at[part], filt.at[part], rows_of, rows_of(me), me, tp, filt_send, filt_recv
         )
+    fetch(0).start()
+    fetch(1).start()
     load_projected.wait()
     load_tables = [
         pltpu.make_async_copy(source, target, load_sem.at[3 + i])
@@ -174,8 +259,8 @@
     ]
     for load in load_tables:
         load.start()
-    load_weight = pltpu.make_async_copy(weight_hbm, weight, load_sem.at[2])
-    load_weight.start()
+    for load in load_weight[1:]:
+        load.start()
     edge.wait()
     halo[...] = jnp.where(me > 0, halo_in[...], 0.0)
 
@@ -247,7 +332,6 @@
     lax.fori_loop(0, GROUPS, filter_step, 0)
 
     def signal_step(group, carry):
-        wait_arrived(signal.at[group], signal_recv.at[group])
         left = forward(lambda i, jb: signal[group, jb, pl.ds(i, CTX, stride=GROUP), :])
         right = spectrum[group_rows(group), :]
         left_real, left_imag = left[:, :256], left[:, 256:]
@@ -284,81 +368,132 @@
         back(1, group)
         return carry
 
-    def return_half(half):
-        for jb in (half, half + 2):
-            chunk = pl.ds(jb, 1)
-            send_slabs(
-                conv.at[chunk], conv_in.at[chunk], rows_of, rows_of(me),
-                me, tp, conv_send.at[jb], conv_recv.at[jb],
-            )
+    def return_chunk(jb):
+        chunk = pl.ds(jb, 1)
+        send_slabs(
+            conv.at[chunk], conv_in.at[chunk], rows_of, rows_of(me),
+            me, tp, conv_send.at[jb], conv_recv.at[jb],
+        )
 
     wait_sent(filt_t, filt_send)
-    lax.fori_loop(0, GROUPS, signal_step, 0)
-    return_half(0)
+    def early_step(group, carry):
+        wait_arrived(signal.at[group], signal_recv.at[group])
+        return signal_step(group, carry)
+
+    lax.fori_loop(0, GROUPS - 1, early_step, 0)
+    wait_arrived(signal.at[GROUPS - 1], signal_recv.at[GROUPS - 1])
+    for part in range(2):
+        fetch(part).wait_recv()
+    share(0)
+    swap(0).start()
+    signal_step(GROUPS - 1, 0)
+    return_chunk(0)
+    return_chunk(2)
+    share(1)
     lax.fori_loop(0, GROUPS, back_step, 0)
-    return_half(1)
-    load_weight.wait()
-
-    def columns(quarter):
-        return pl.ds(pl.multiple_of(quarter * 1024, 1024), 1024)
-
-    def to_far(jb, side):
-        half = slice(512 * side, 512 * side + 512)
-        return pltpu.make_async_remote_copy(
-            src_ref=far(jb).at[:, half],
-            dst_ref=far_in.at[jb, :, half],
-            send_sem=far_send.at[jb, side],
-            recv_sem=far_recv.at[jb, side],
-            device_id=(me, (up, down)[side]),
-            device_id_type=MESH,
-        )
-
-    def to_near(jb, side):
-        return pltpu.make_async_remote_copy(
-            src_ref=near(jb, side),
-            dst_ref=near_in.at[jb, side],
-            send_sem=near_send.at[jb, side],
-            recv_sem=near_recv.at[jb, side],
-            device_id=(me, (up, down)[side]),
-            device_id_type=MESH,
-        )
-
-    def compute(jb):
+    return_chunk(1)
+    return_chunk(3)
+    for load in load_weight[1:]:
+        load.wait()
+    for part in range(2):
+        fetch(part).wait_send()
+
+    def gather(jb):
+        return to_tp(
+            gather_out(jb), gather_in.at[jb], partner, gather_send.at[jb], gather_recv.at[jb]
+        )
+
+    def send_sum(jb):
+        return to_tp(sum_out(jb), sum_in.at[jb], mate, sum_send.at[jb], sum_recv.at[jb])
+
+    def gate_chunk(jb):
         wait_arrived(conv_in.at[pl.ds(jb, 1)], conv_recv.at[jb])
         tokens = slice(jb * 128, jb * 128 + 128)
         mixed = conv_in[jb].T + skip_gain[...] * gated[tokens, :]
-        gated_out[...] = (shortened_q[tokens, :] * mixed).astype(BF16)
-        far(jb)[...] = dot(gated_out[...], weight[:, columns(lax.rem(tp + 2, TP))])
-        to_far(jb, 0).start()
-        to_far(jb, 1).start()
-        near(jb, 0)[...] = dot(gated_out[...], weight[:, columns(up)])
-        near(jb, 1)[...] = dot(gated_out[...], weight[:, columns(down)])
-        out[tokens, :] = dot(gated_out[...], weight[:, columns(tp)])
-
-    def relay(jb):
-        for side in (0, 1):
-            half = slice(512 * side, 512 * side + 512)
-            to_far(jb, side).wait_recv()
-            near(jb, side)[:, half] += far_in[jb, :, half]
-            to_near(jb, side).start()
-
-    order = (0, 2, 1, 3)
-    compute(order[0])
-    for step in range(1, 4):
-        compute(order[step])
-        relay(order[step - 1])
-    relay(order[3])
-    for jb in order:
-        tokens = slice(jb * 128, jb * 128 + 128)
-        to_near(jb, 0).wait_recv()
-        to_near(jb, 1).wait_recv()
-        out[tokens, :] += near_in[jb, 0] + near_in[jb, 1]
+        gated_out[jb] = (shortened_q[tokens, :] * mixed).astype(BF16)
+
+    def start_gather(jb):
+        gather_out(jb)[...] = gated_out[jb].astype(F32)
+        gather(jb).start()
+
+    def project(jb):
+        gather(jb).wait_recv()
+        partner_out[...] = gather_in[jb].astype(BF16)
+        sum_out(jb)[...] = dot(gated_out[jb], weight[:, columns(mate)]) + dot(
+            partner_out[...], partner_weight[:, 1024:]
+        )
+        send_sum(jb).start()
+        out[jb * 128 : jb * 128 + 128, :] = dot(gated_out[jb], weight[:, columns(tp)]) + dot(
+            partner_out[...], partner_weight[:, :1024]
+        )
+
+    def finish(jb):
+        send_sum(jb).wait_recv()
+        out[jb * 128 : jb * 128 + 128, :] += sum_in[jb]
+
+    halves = (slice(0, 512), slice(512, 1024))
+
+    def to_far(side):
+        return to_tp(
+            far.at[:, halves[1 - side]], far_in.at[:, halves[1 - side]],
+            (mate, partner)[side], far_send.at[side], far_recv.at[side],
+        )
+
+    def to_near(side):
+        return to_tp(
+            near[side], near_in[side], (mate, partner)[side], near_send.at[side], near_recv.at[side]
+        )
+
+    def relay(side):
+        to_far(1 - side).wait_recv()
+        near[side][:, halves[side]] += far_in[:, halves[side]]
+        to_near(side).start()
+
+    gate_chunk(0)
+    far[...] = dot(gated_out[0], weight[:, columns(lax.rem(tp + 2, TP))])
+    to_far(0).start()
+    to_far(1).start()
+    near[0][...] = dot(gated_out[0], weight[:, columns(mate)])
+    near[1][...] = dot(gated_out[0], weight[:, columns(partner)])
+    out[0:128, :] = dot(gated_out[0], weight[:, columns(tp)])
+    gate_chunk(2)
+    start_gather(2)
+    relay(0)
+    for part in range(2):
+        pltpu.make_async_copy(share_bytes(), share_bytes(), share_recv.at[part]).wait()
+    swap(1).start()
+    swap(0).wait_recv()
+    round_quarters(0)
+    gate_chunk(1)
+    swap(1).wait_recv()
+    round_quarters(1)
+    gather(2).wait_send()
+    start_gather(1)
+    project(2)
+    gate_chunk(3)
+    gather(1).wait_send()
+    start_gather(3)
+    project(1)
+    gather(3).wait_send()
+    relay(1)
+    project(3)
+    finish(2)
+    finish(1)
+    to_near(0).wait_recv()
+    to_near(1).wait_recv()
+    out[0:128, :] += near_in[0][...] + near_in[1][...]
+    finish(3)
+    for side in range(2):
+        to_far(side).wait_send()
+        to_near(side).wait_send()
     wait_sent(gated_t, signal_send)
+    for part in range(2):
+        pltpu.make_async_copy(share_bytes(), share_bytes(), share_send.at[part]).wait()
+        swap(part).wait_send()
     for jb in range(4):
         wait_sent(conv.at[pl.ds(jb, 1)], conv_send.at[jb])
-        for side in (0, 1):
-            to_far(jb, side).wait_send()
-            to_near(jb, side).wait_send()
+        if jb:
+            send_sum(jb).wait_send()
 
 
 VMEM = pl.BlockSpec(memory_space=pltpu.VMEM)
@@ -391,10 +526,14 @@
             pltpu.VMEM((GROUP * 64, 1536), BF16),
             pltpu.VMEM((OWN * 64, 512), F32),
             pltpu.VMEM((4, 1024, 128), F32),
+            pltpu.VMEM((4, 128, 1024), BF16),
             pltpu.VMEM((128, 1024), BF16),
+            pltpu.VMEM((1024, 2048), F32),
+            pltpu.VMEM((1024, 2048), BF16),
             pltpu.VMEM((4, 128, 1024), F32),
-            pltpu.VMEM((4, 2, 128, 1024), F32),
-            DMA((8,)),
+            pltpu.VMEM((4, 128, 1024), F32),
+            pltpu.VMEM((128, 1024), F32),
+            DMA((12,)),
             DMA,
             DMA,
             DMA,
@@ -403,10 +542,20 @@
             DMA((GROUPS,)),
             DMA((4,)),
             DMA((4,)),
-            DMA((4, 2)),
-            DMA((4, 2)),
-            DMA((4, 2)),
-            DMA((4, 2)),
+            DMA((2,)),
+            DMA((2,)),
+            DMA((2,)),
+            DMA((2,)),
+            DMA((2,)),
+            DMA((2,)),
+            DMA((4,)),
+            DMA((4,)),
+            DMA((4,)),
+            DMA((4,)),
+            DMA((2,)),
+            DMA((2,)),
+            DMA((2,)),
+            DMA((2,)),
         ],
         compiler_params=pltpu.CompilerParams(
             collective_id=0, has_side_effects=True, vmem_limit_bytes=60 * 2**20

time: 147 us -> 139 us (0.946)
  Pallas kernels: 141 us -> 134 us
    pallas_call x1, Pallas kernels: 141 us -> 134 us  [per_device(): pl.pallas_call(mixer_kernel, out_shape=jax.ShapeDtypeStruct((512, 1024),...]
where the time goes in v4:
time: 139 us; the launch traced here: 137 us
  Pallas kernels  134 us (96%)
  local copies, waits for them, and re-layouts  3.16 us (2%)
    pallas_call x1, Pallas kernels, per_device(): pl.pallas_call(mixer_kernel, out_shape=jax.ShapeDtypeStruct((512, 1024),...  134 us
    unnamed x1, local copies, waits for them, and re-layouts  3.16 us

profile of v4, /device:TPU:64, one launch (start us, length us, event | category | flops | bytes accessed | tf_op | source)
XLA Modules:
  0.0 137.1 jit_solution(18259494250422315058)
XLA Ops:
  0.0 133.9 %mixer.1 = f32[512,1024]{1,0:T(8,128)} custom-call(f32[3,512,1024]{2,1,0:T(8,128)} %projected_hbm.1, f32[3,3,1024]{2,1,0:T(4,128)} %short_filters.1, f32[512,1024]{1,0:T(8,128)} %long_filter_hbm.1, f32[1,1024]{1,0:T(1,128)} %bitcast.1, bf16[1024,4096]{1,0:T(8,128)(2,1)} %weight_hbm.1, bf16[128,192]{1,0:T(8,128)(2,1)} %constant.10.clone.first_hbm, ...), custom_call_target="tpu_custom_call" | custom-call | tf_op jit(solution)/shard_map/mixer/pallas_call | solution.py:505
  134.0 3.2 %copy.12 = f32[512,1024]{1,0:T(8,128)} copy(f32[512,1024]{1,0:T(8,128)} %mixer.1) | data formatting | bytes 4194304

commit v5 on v4

--- a/solution.py
+++ b/solution.py
@@ -156,7 +156,7 @@
 
     def share(part):
         for direction, offset in enumerate(((1, 0, 0), (3, 0, 0), (0, 1, 0), (0, 3, 0))):
-            first_row = mine * 256 + direction * 64 + part * 32
+            first_row = mine * 256 + part * 128 + direction * 32
             slab = weight_in.at[pl.ds(pl.multiple_of(first_row, 32), 32), :]
             pltpu.make_async_remote_copy(
                 src_ref=slab,
@@ -167,11 +167,11 @@
                 device_id_type=MESH,
             ).start()
 
-    def share_bytes():
-        return weight_in.at[pl.ds(pl.multiple_of(theirs * 256, 256), 128), :]
+    def shared(quarter, part):
+        return weight_in.at[pl.ds(pl.multiple_of(quarter * 256 + part * 128, 128), 128), :]
 
     def swap(which):
-        slab = weight_in.at[quarter_rows((mine, theirs)[which]), :]
+        slab = weight_in.at[quarter_rows(mine), :] if which == 2 else shared(theirs, which)
         return pltpu.make_async_remote_copy(
             src_ref=slab,
             dst_ref=slab,
@@ -368,10 +368,14 @@
         back(1, group)
         return carry
 
-    def return_chunk(jb):
+    def return_chunk(jb, first_row=0, count=OWN):
         chunk = pl.ds(jb, 1)
+
+        def slab(device):
+            return pl.ds(pl.multiple_of(device * OWN + first_row, GROUP), count)
+
         send_slabs(
-            conv.at[chunk], conv_in.at[chunk], rows_of, rows_of(me),
+            conv.at[chunk], conv_in.at[chunk], slab, slab(me),
             me, tp, conv_send.at[jb], conv_recv.at[jb],
         )
 
@@ -381,30 +385,34 @@
         return signal_step(group, carry)
 
     lax.fori_loop(0, GROUPS - 1, early_step, 0)
+    return_chunk(0, 0, OWN - GROUP)
     wait_arrived(signal.at[GROUPS - 1], signal_recv.at[GROUPS - 1])
     for part in range(2):
         fetch(part).wait_recv()
+    swap(2).start()
+    signal_step(GROUPS - 1, 0)
+    return_chunk(0, OWN - GROUP, GROUP)
+    return_chunk(2)
     share(0)
-    swap(0).start()
-    signal_step(GROUPS - 1, 0)
-    return_chunk(0)
-    return_chunk(2)
     share(1)
-    lax.fori_loop(0, GROUPS, back_step, 0)
-    return_chunk(1)
-    return_chunk(3)
     for load in load_weight[1:]:
         load.wait()
     for part in range(2):
         fetch(part).wait_send()
 
-    def gather(jb):
+    def gather(jb, half):
+        tokens = pl.ds(64 * half, 64)
         return to_tp(
-            gather_out(jb), gather_in.at[jb], partner, gather_send.at[jb], gather_recv.at[jb]
-        )
-
-    def send_sum(jb):
-        return to_tp(sum_out(jb), sum_in.at[jb], mate, sum_send.at[jb], sum_recv.at[jb])
+            gather_out(jb).at[tokens, :], gather_in.at[jb, tokens, :],
+            partner, gather_send.at[jb, half], gather_recv.at[jb, half],
+        )
+
+    def send_sum(jb, half):
+        tokens = pl.ds(64 * half, 64)
+        return to_tp(
+            sum_out(jb).at[tokens, :], sum_in.at[jb, tokens, :],
+            mate, sum_send.at[jb, half], sum_recv.at[jb, half],
+        )
 
     def gate_chunk(jb):
         wait_arrived(conv_in.at[pl.ds(jb, 1)], conv_recv.at[jb])
@@ -414,22 +422,33 @@
 
     def start_gather(jb):
         gather_out(jb)[...] = gated_out[jb].astype(F32)
-        gather(jb).start()
-
-    def project(jb):
-        gather(jb).wait_recv()
-        partner_out[...] = gather_in[jb].astype(BF16)
-        sum_out(jb)[...] = dot(gated_out[jb], weight[:, columns(mate)]) + dot(
-            partner_out[...], partner_weight[:, 1024:]
-        )
-        send_sum(jb).start()
+        for half in range(2):
+            gather(jb, half).start()
+
+    def gather_sent(jb):
+        for half in range(2):
+            gather(jb, half).wait_send()
+
+    def push_sums(jb):
+        for half in range(2):
+            tokens = slice(64 * half, 64 * half + 64)
+            gather(jb, half).wait_recv()
+            partner_out[tokens, :] = gather_in[jb, tokens, :].astype(BF16)
+            sum_out(jb)[tokens, :] = dot(gated_out[jb, tokens, :], weight[:, columns(mate)]) + dot(
+                partner_out[tokens, :], partner_weight[:, 1024:]
+            )
+            send_sum(jb, half).start()
+
+    def keep_sums(jb):
         out[jb * 128 : jb * 128 + 128, :] = dot(gated_out[jb], weight[:, columns(tp)]) + dot(
             partner_out[...], partner_weight[:, :1024]
         )
 
     def finish(jb):
-        send_sum(jb).wait_recv()
-        out[jb * 128 : jb * 128 + 128, :] += sum_in[jb]
+        for half in range(2):
+            tokens = slice(64 * half, 64 * half + 64)
+            send_sum(jb, half).wait_recv()
+            out[jb * 128 + 64 * half : jb * 128 + 64 * half + 64, :] += sum_in[jb, tokens, :]
 
     halves = (slice(0, 512), slice(512, 1024))
 
@@ -453,47 +472,55 @@
     far[...] = dot(gated_out[0], weight[:, columns(lax.rem(tp + 2, TP))])
     to_far(0).start()
     to_far(1).start()
+    lax.fori_loop(0, GROUPS, back_step, 0)
+    return_chunk(1)
+    return_chunk(3)
     near[0][...] = dot(gated_out[0], weight[:, columns(mate)])
-    near[1][...] = dot(gated_out[0], weight[:, columns(partner)])
-    out[0:128, :] = dot(gated_out[0], weight[:, columns(tp)])
     gate_chunk(2)
     start_gather(2)
     relay(0)
+    near[1][...] = dot(gated_out[0], weight[:, columns(partner)])
+    out[0:128, :] = dot(gated_out[0], weight[:, columns(tp)])
+    swap(2).wait_recv()
+    round_quarters(0)
     for part in range(2):
-        pltpu.make_async_copy(share_bytes(), share_bytes(), share_recv.at[part]).wait()
-    swap(1).start()
-    swap(0).wait_recv()
-    round_quarters(0)
+        wait_arrived(shared(theirs, part), share_recv.at[part])
+        swap(part).start()
+    for part in range(2):
+        swap(part).wait_recv()
+    round_quarters(1)
     gate_chunk(1)
-    swap(1).wait_recv()
-    round_quarters(1)
-    gather(2).wait_send()
+    gather_sent(2)
     start_gather(1)
-    project(2)
+    push_sums(2)
+    keep_sums(2)
     gate_chunk(3)
-    gather(1).wait_send()
+    gather_sent(1)
     start_gather(3)
-    project(1)
-    gather(3).wait_send()
+    push_sums(1)
+    keep_sums(1)
+    gather_sent(3)
     relay(1)
-    project(3)
-    finish(2)
-    finish(1)
+    push_sums(3)
+    keep_sums(3)
     to_near(0).wait_recv()
     to_near(1).wait_recv()
     out[0:128, :] += near_in[0][...] + near_in[1][...]
-    finish(3)
+    for jb in (2, 1, 3):
+        finish(jb)
     for side in range(2):
         to_far(side).wait_send()
         to_near(side).wait_send()
     wait_sent(gated_t, signal_send)
     for part in range(2):
-        pltpu.make_async_copy(share_bytes(), share_bytes(), share_send.at[part]).wait()
+        wait_arrived(shared(mine, part), share_send.at[part])
         swap(part).wait_send()
+    swap(2).wait_send()
     for jb in range(4):
         wait_sent(conv.at[pl.ds(jb, 1)], conv_send.at[jb])
         if jb:
-            send_sum(jb).wait_send()
+            for half in range(2):
+                send_sum(jb, half).wait_send()
 
 
 VMEM = pl.BlockSpec(memory_space=pltpu.VMEM)
@@ -546,12 +573,12 @@
             DMA((2,)),
             DMA((2,)),
             DMA((2,)),
-            DMA((2,)),
-            DMA((2,)),
-            DMA((4,)),
-            DMA((4,)),
-            DMA((4,)),
-            DMA((4,)),
+            DMA((3,)),
+            DMA((3,)),
+            DMA((4, 2)),
+            DMA((4, 2)),
+            DMA((4, 2)),
+            DMA((4, 2)),
             DMA((2,)),
             DMA((2,)),
             DMA((2,)),

time: 139 us -> 134 us (0.964); the launches traced: 137 us -> 134 us
  Pallas kernels: 134 us -> 131 us
    pallas_call x1, Pallas kernels: 134 us -> 131 us  [per_device(): pl.pallas_call(mixer_kernel, out_shape=jax.ShapeDtypeStruct((512, 1024),...]
where the time goes in v5:
time: 134 us
  Pallas kernels  131 us (98%)
  local copies, waits for them, and re-layouts  3.16 us (2%)
    pallas_call x1, Pallas kernels, per_device(): pl.pallas_call(mixer_kernel, out_shape=jax.ShapeDtypeStruct((512, 1024),...  131 us
    unnamed x1, local copies, waits for them, and re-layouts  3.16 us

profile of v5, /device:TPU:64, one launch (start us, length us, event | category | flops | bytes accessed | tf_op | source)
XLA Modules:
  0.0 134.2 jit_solution(9588718796746643378)
XLA Ops:
  0.0 131.1 %mixer.1 = f32[512,1024]{1,0:T(8,128)} custom-call(f32[3,512,1024]{2,1,0:T(8,128)} %projected_hbm.1, f32[3,3,1024]{2,1,0:T(4,128)} %short_filters.1, f32[512,1024]{1,0:T(8,128)} %long_filter_hbm.1, f32[1,1024]{1,0:T(1,128)} %bitcast.1, bf16[1024,4096]{1,0:T(8,128)(2,1)} %weight_hbm.1, bf16[128,192]{1,0:T(8,128)(2,1)} %constant.10.clone.first_hbm, ...), custom_call_target="tpu_custom_call" | custom-call | tf_op jit(solution)/shard_map/mixer/pallas_call | solution.py:532
  131.1 3.2 %copy.12 = f32[512,1024]{1,0:T(8,128)} copy(f32[512,1024]{1,0:T(8,128)} %mixer.1) | data formatting | bytes 4194304

commit v6 on v5

--- a/solution.py
+++ b/solution.py
@@ -103,14 +103,15 @@
 def mixer_kernel(
     projected_hbm, short_filters, long_filter_hbm, skip_gain, weight_hbm,
     first_hbm, twist_hbm, second_hbm, back_second_hbm, back_first_hbm,
-    out,
+    kept_hbm, sum_in, near_in_partner,
+    kept,
     projected, long_filter, weight, first, twist, second, back_second, back_first,
     halo, halo_in, filt_t, gated_t, filt, signal,
     shortened_q, rows, spectrum, conv_in, gated_out, partner_out, weight_in, partner_weight,
-    gather_in, sum_in, near_in_partner,
+    gather_in,
     load_sem, halo_send, halo_recv, filt_send, filt_recv, signal_send, signal_recv,
     conv_send, conv_recv, fetch_send, fetch_recv, share_send, share_recv, swap_send, swap_recv,
-    gather_send, gather_recv, sum_send, sum_recv, far_send, far_recv, near_send, near_recv,
+    gather_send, gather_recv, sum_send, sum_recv, far_send, far_recv, near_send, near_recv, kept_sem,
 ):
     me = lax.axis_index("ctx")
     tp = lax.axis_index("tp")
@@ -119,7 +120,7 @@
     mine, theirs = 2 * parity + me % 2, 2 * (1 - parity) + me % 2
     conv = filt_t
     gated = long_filter
-    fetch_out = out
+    fetch_out = kept
 
     def sum_out(jb):
         return projected.at[0, pl.ds(jb * 128, 128), :]
@@ -154,10 +155,18 @@
             partner, fetch_send.at[part], fetch_recv.at[part],
         )
 
+    def fetch_rest(part):
+        rest = pl.ds(pl.multiple_of(theirs * 256 + 192, 64), 64)
+        return to_tp(
+            projected.at[2, pl.ds(part * 64, 64), :],
+            weight_in.at[rest, pl.ds(part * 1024, 1024)],
+            partner, fetch_send.at[2 + part], fetch_recv.at[2 + part],
+        )
+
     def share(part):
         for direction, offset in enumerate(((1, 0, 0), (3, 0, 0), (0, 1, 0), (0, 3, 0))):
-            first_row = mine * 256 + part * 128 + direction * 32
-            slab = weight_in.at[pl.ds(pl.multiple_of(first_row, 32), 32), :]
+            first_row = mine * 256 + (128 + direction * 16 if part else direction * 32)
+            slab = weight_in.at[pl.ds(pl.multiple_of(first_row, 16), 16 if part else 32), :]
             pltpu.make_async_remote_copy(
                 src_ref=slab,
                 dst_ref=slab,
@@ -168,10 +177,11 @@
             ).start()
 
     def shared(quarter, part):
-        return weight_in.at[pl.ds(pl.multiple_of(quarter * 256 + part * 128, 128), 128), :]
+        first_row, count = ((0, 128), (128, 64), (192, 64))[part]
+        return weight_in.at[pl.ds(pl.multiple_of(quarter * 256 + first_row, 64), count), :]
 
     def swap(which):
-        slab = weight_in.at[quarter_rows(mine), :] if which == 2 else shared(theirs, which)
+        slab = weight_in.at[quarter_rows(mine), :] if which == 3 else shared(theirs, which)
         return pltpu.make_async_remote_copy(
             src_ref=slab,
             dst_ref=slab,
@@ -297,6 +307,12 @@
         return carry
 
     lax.fori_loop(0, 8, query, 0)
+
+    load_weight[2].wait()
+    for part, quarter in enumerate((partner, TP - 1 - partner)):
+        rest = pl.ds(pl.multiple_of(theirs * 256 + 192, 64), 64)
+        projected[2, part * 64 : part * 64 + 64, :] = weight[rest, columns(quarter)].astype(F32)
+        fetch_rest(part).start()
 
     for load in load_tables:
         load.wait()
@@ -389,16 +405,19 @@
     wait_arrived(signal.at[GROUPS - 1], signal_recv.at[GROUPS - 1])
     for part in range(2):
         fetch(part).wait_recv()
-    swap(2).start()
+    swap(3).start()
     signal_step(GROUPS - 1, 0)
     return_chunk(0, OWN - GROUP, GROUP)
     return_chunk(2)
     share(0)
     share(1)
-    for load in load_weight[1:]:
-        load.wait()
+    load_weight[1].wait()
+    load_weight[3].wait()
     for part in range(2):
         fetch(part).wait_send()
+        fetch_rest(part).wait_send()
+        fetch_rest(part).wait_recv()
+    swap(2).start()
 
     def gather(jb, half):
         tokens = pl.ds(64 * half, 64)
@@ -440,15 +459,16 @@
             send_sum(jb, half).start()
 
     def keep_sums(jb):
-        out[jb * 128 : jb * 128 + 128, :] = dot(gated_out[jb], weight[:, columns(tp)]) + dot(
+        kept[jb * 128 : jb * 128 + 128, :] = dot(gated_out[jb], weight[:, columns(tp)]) + dot(
             partner_out[...], partner_weight[:, :1024]
         )
-
-    def finish(jb):
-        for half in range(2):
-            tokens = slice(64 * half, 64 * half + 64)
-            send_sum(jb, half).wait_recv()
-            out[jb * 128 + 64 * half : jb * 128 + 64 * half + 64, :] += sum_in[jb, tokens, :]
+        store(jb).start()
+
+    def store(jb):
+        tokens = pl.ds(jb * 128, 128)
+        return pltpu.make_async_copy(
+            kept.at[tokens, :], kept_hbm.at[tokens, :], kept_sem.at[jb]
+        )
 
     halves = (slice(0, 512), slice(512, 1024))
 
@@ -458,35 +478,42 @@
             (mate, partner)[side], far_send.at[side], far_recv.at[side],
         )
 
-    def to_near(side):
+    def to_near(side, part):
+        half = halves[side] if part else halves[1 - side]
         return to_tp(
-            near[side], near_in[side], (mate, partner)[side], near_send.at[side], near_recv.at[side]
+            near[side].at[:, half], near_in[side].at[:, half],
+            (mate, partner)[side], near_send.at[side, part], near_recv.at[side, part],
         )
 
     def relay(side):
         to_far(1 - side).wait_recv()
         near[side][:, halves[side]] += far_in[:, halves[side]]
-        to_near(side).start()
+        to_near(side, 1).start()
 
     gate_chunk(0)
-    far[...] = dot(gated_out[0], weight[:, columns(lax.rem(tp + 2, TP))])
-    to_far(0).start()
-    to_far(1).start()
+    for side in range(2):
+        first_column = lax.rem(tp + 2, TP) * 1024 + 512 * (1 - side)
+        far[:, halves[1 - side]] = dot(
+            gated_out[0], weight[:, pl.ds(pl.multiple_of(first_column, 512), 512)]
+        )
+        to_far(side).start()
+    near[0][...] = dot(gated_out[0], weight[:, columns(mate)])
+    to_near(0, 0).start()
     lax.fori_loop(0, GROUPS, back_step, 0)
     return_chunk(1)
     return_chunk(3)
-    near[0][...] = dot(gated_out[0], weight[:, columns(mate)])
     gate_chunk(2)
     start_gather(2)
     relay(0)
     near[1][...] = dot(gated_out[0], weight[:, columns(partner)])
-    out[0:128, :] = dot(gated_out[0], weight[:, columns(tp)])
-    swap(2).wait_recv()
+    kept[0:128, :] = dot(gated_out[0], weight[:, columns(tp)])
+    store(0).start()
+    swap(3).wait_recv()
     round_quarters(0)
     for part in range(2):
         wait_arrived(shared(theirs, part), share_recv.at[part])
         swap(part).start()
-    for part in range(2):
+    for part in range(3):
         swap(part).wait_recv()
     round_quarters(1)
     gate_chunk(1)
@@ -500,27 +527,52 @@
     push_sums(1)
     keep_sums(1)
     gather_sent(3)
+    to_near(1, 0).start()
     relay(1)
     push_sums(3)
     keep_sums(3)
-    to_near(0).wait_recv()
-    to_near(1).wait_recv()
-    out[0:128, :] += near_in[0][...] + near_in[1][...]
-    for jb in (2, 1, 3):
-        finish(jb)
     for side in range(2):
         to_far(side).wait_send()
-        to_near(side).wait_send()
+        for part in range(2):
+            to_near(side, part).wait()
+    for jb in range(4):
+        store(jb).wait()
+        if jb:
+            for half in range(2):
+                send_sum(jb, half).wait()
     wait_sent(gated_t, signal_send)
     for part in range(2):
         wait_arrived(shared(mine, part), share_send.at[part])
         swap(part).wait_send()
     swap(2).wait_send()
+    swap(3).wait_send()
     for jb in range(4):
         wait_sent(conv.at[pl.ds(jb, 1)], conv_send.at[jb])
-        if jb:
-            for half in range(2):
-                send_sum(jb, half).wait_send()
+
+
+def add_kernel(kept, landed, landed_chunk, total, left, right, first_chunk, load_sem, store_sem):
+    chunks = [pl.ds(128 * jb, 128) for jb in range(4)]
+    loads = [pltpu.make_async_copy(landed_chunk, first_chunk, load_sem.at[8])]
+    for jb, chunk in enumerate(chunks):
+        loads.append(pltpu.make_async_copy(kept.at[chunk, :], left.at[chunk, :], load_sem.at[jb]))
+        loads.append(
+            pltpu.make_async_copy(landed.at[chunk, :], right.at[chunk, :], load_sem.at[4 + jb])
+        )
+    for load in loads:
+        load.start()
+    loads[0].wait()
+    stores = []
+    for jb, chunk in enumerate(chunks):
+        loads[1 + 2 * jb].wait()
+        loads[2 + 2 * jb].wait()
+        value = left[chunk, :] + right[chunk, :]
+        left[chunk, :] = value + first_chunk[...] if jb == 0 else value
+        stores.append(
+            pltpu.make_async_copy(left.at[chunk, :], total.at[chunk, :], store_sem.at[jb])
+        )
+        stores[jb].start()
+    for store in stores:
+        store.wait()
 
 
 VMEM = pl.BlockSpec(memory_space=pltpu.VMEM)
@@ -529,12 +581,17 @@
 
 
 def per_device(projected, short_filters, long_filter, skip_gain, out_weight):
-    return pl.pallas_call(
+    kept, landed, landed_chunk = pl.pallas_call(
         mixer_kernel,
-        out_shape=jax.ShapeDtypeStruct((512, 1024), F32),
+        out_shape=(
+            jax.ShapeDtypeStruct((512, 1024), F32),
+            jax.ShapeDtypeStruct((4, 128, 1024), F32),
+            jax.ShapeDtypeStruct((128, 1024), F32),
+        ),
         in_specs=[HBM, VMEM, HBM, VMEM, HBM] + [HBM] * 5,
-        out_specs=VMEM,
+        out_specs=(HBM, HBM, HBM),
         scratch_shapes=[
+            pltpu.VMEM((512, 1024), F32),
             pltpu.VMEM((3, 512, 1024), F32),
             pltpu.VMEM((512, 1024), F32),
             pltpu.VMEM((1024, 4096), BF16),
@@ -558,8 +615,6 @@
             pltpu.VMEM((1024, 2048), F32),
             pltpu.VMEM((1024, 2048), BF16),
             pltpu.VMEM((4, 128, 1024), F32),
-            pltpu.VMEM((4, 128, 1024), F32),
-            pltpu.VMEM((128, 1024), F32),
             DMA((12,)),
             DMA,
             DMA,
@@ -569,20 +624,21 @@
             DMA((GROUPS,)),
             DMA((4,)),
             DMA((4,)),
+            DMA((4,)),
+            DMA((4,)),
             DMA((2,)),
             DMA((2,)),
-            DMA((2,)),
-            DMA((2,)),
-            DMA((3,)),
-            DMA((3,)),
+            DMA((4,)),
+            DMA((4,)),
             DMA((4, 2)),
             DMA((4, 2)),
             DMA((4, 2)),
             DMA((4, 2)),
             DMA((2,)),
             DMA((2,)),
-            DMA((2,)),
-            DMA((2,)),
+            DMA((2, 2)),
+            DMA((2, 2)),
+            DMA((4,)),
         ],
         compiler_params=pltpu.CompilerParams(
             collective_id=0, has_side_effects=True, vmem_limit_bytes=60 * 2**20
@@ -592,6 +648,21 @@
         projected, short_filters, long_filter, skip_gain[None], out_weight,
         *[jnp.asarray(table) for table in tables()],
     )
+    return pl.pallas_call(
+        add_kernel,
+        out_shape=jax.ShapeDtypeStruct((512, 1024), F32),
+        in_specs=[HBM] * 3,
+        out_specs=HBM,
+        scratch_shapes=[
+            pltpu.VMEM((512, 1024), F32),
+            pltpu.VMEM((512, 1024), F32),
+            pltpu.VMEM((128, 1024), F32),
+            DMA((9,)),
+            DMA((4,)),
+        ],
+        compiler_params=pltpu.CompilerParams(vmem_limit_bytes=60 * 2**20),
+        name="add",
+    )(kept, landed.reshape(512, 1024), landed_chunk)
 
 
 def solution(mesh):

time: 134 us -> 131 us (0.978)
  local copies, waits for them, and re-layouts: 3.16 us -> 0 us
    unnamed x1 -> x0, local copies, waits for them, and re-layouts: 3.16 us -> none
    pallas_call x1 -> x2, Pallas kernels: 131 us -> 130 us  [the longest x1 127 us: per_device(): pl.pallas_call(mixer_kernel, out_shape=(jax.ShapeDtypeStruct((512, 1024),...]
where the time goes in v6:
time: 131 us
  Pallas kernels  130 us (99%)
    pallas_call x1, Pallas kernels, per_device(): pl.pallas_call(mixer_kernel, out_shape=(jax.ShapeDtypeStruct((512, 1024),...  127 us
    pallas_call x1, Pallas kernels, per_device(): pl.pallas_call(add_kernel, out_shape=jax.ShapeDtypeStruct((512, 1024), F3...  3.26 us

profile of v6, /device:TPU:64, one launch (start us, length us, event | category | flops | bytes accessed | tf_op | source)
XLA Modules:
  0.0 130.6 jit_solution(17619433716898524839)
XLA Ops:
  0.0 127.2 %mixer.1 = (f32[512,1024]{1,0:T(8,128)}, f32[4,128,1024]{2,1,0:T(8,128)}, f32[128,1024]{1,0:T(8,128)}) custom-call(f32[3,512,1024]{2,1,0:T(8,128)} %projected_hbm.1, f32[3,3,1024]{2,1,0:T(4,128)} %short_filters.1, f32[512,1024]{1,0:T(8,128)} %long_filter_hbm.1, f32[1,1024]{1,0:T(1,128)} %bitcast.3, bf16[1024,4096]{1,0:T(8,128)(2,1)} %weight_hbm.1, ...), custom_call_target="tpu_custom_call" | custom-call | tf_op jit(solution)/shard_map/mixer/pallas_call | solution.py:584
  127.2 3.3 %add.1 = f32[512,1024]{1,0:T(8,128)} custom-call(f32[512,1024]{1,0:T(8,128)} %get-tuple-element.8.kept, f32[512,1024]{1,0:T(8,128)} %bitcast.2, f32[128,1024]{1,0:T(8,128)} %get-tuple-element.10.landed_chunk), custom_call_target="tpu_custom_call" | custom-call | tf_op jit(solution)/shard_map/add/pallas_call | solution.py:651

commit v7 on v6

--- a/solution.py
+++ b/solution.py
@@ -438,9 +438,10 @@
         tokens = slice(jb * 128, jb * 128 + 128)
         mixed = conv_in[jb].T + skip_gain[...] * gated[tokens, :]
         gated_out[jb] = (shortened_q[tokens, :] * mixed).astype(BF16)
+        if jb:
+            gather_out(jb)[...] = gated_out[jb].astype(F32)
 
     def start_gather(jb):
-        gather_out(jb)[...] = gated_out[jb].astype(F32)
         for half in range(2):
             gather(jb, half).start()
 
@@ -448,15 +449,14 @@
         for half in range(2):
             gather(jb, half).wait_send()
 
-    def push_sums(jb):
-        for half in range(2):
-            tokens = slice(64 * half, 64 * half + 64)
-            gather(jb, half).wait_recv()
-            partner_out[tokens, :] = gather_in[jb, tokens, :].astype(BF16)
-            sum_out(jb)[tokens, :] = dot(gated_out[jb, tokens, :], weight[:, columns(mate)]) + dot(
-                partner_out[tokens, :], partner_weight[:, 1024:]
-            )
-            send_sum(jb, half).start()
+    def push_sums(jb, half):
+        tokens = slice(64 * half, 64 * half + 64)
+        gather(jb, half).wait_recv()
+        partner_out[tokens, :] = gather_in[jb, tokens, :].astype(BF16)
+        sum_out(jb)[tokens, :] = dot(gated_out[jb, tokens, :], weight[:, columns(mate)]) + dot(
+            partner_out[tokens, :], partner_weight[:, 1024:]
+        )
+        send_sum(jb, half).start()
 
     def keep_sums(jb):
         kept[jb * 128 : jb * 128 + 128, :] = dot(gated_out[jb], weight[:, columns(tp)]) + dot(
@@ -516,21 +516,24 @@
     for part in range(3):
         swap(part).wait_recv()
     round_quarters(1)
+    to_near(1, 0).start()
     gate_chunk(1)
     gather_sent(2)
     start_gather(1)
-    push_sums(2)
+    push_sums(2, 0)
+    push_sums(2, 1)
     keep_sums(2)
     gate_chunk(3)
+    push_sums(1, 0)
     gather_sent(1)
     start_gather(3)
-    push_sums(1)
+    push_sums(1, 1)
     keep_sums(1)
+    push_sums(3, 0)
+    relay(1)
+    push_sums(3, 1)
+    keep_sums(3)
     gather_sent(3)
-    to_near(1, 0).start()
-    relay(1)
-    push_sums(3)
-    keep_sums(3)
     for side in range(2):
         to_far(side).wait_send()
         for part in range(2):

time: 131 us -> 131 us (level)
  no operation moved by 1% of the time
where the time goes in v7:
time: 131 us; the launch traced here: 130 us
  Pallas kernels  130 us (99%)
    pallas_call x1, Pallas kernels, per_device(): pl.pallas_call(mixer_kernel, out_shape=(jax.ShapeDtypeStruct((512, 1024),...  127 us
    pallas_call x1, Pallas kernels, per_device(): pl.pallas_call(add_kernel, out_shape=jax.ShapeDtypeStruct((512, 1024), F3...  3.26 us

profile of v7, /device:TPU:64, one launch (start us, length us, event | category | flops | bytes accessed | tf_op | source)
XLA Modules:
  0.0 130.5 jit_solution(9921439921119623262)
XLA Ops:
  0.0 127.1 %mixer.1 = (f32[512,1024]{1,0:T(8,128)}, f32[4,128,1024]{2,1,0:T(8,128)}, f32[128,1024]{1,0:T(8,128)}) custom-call(f32[3,512,1024]{2,1,0:T(8,128)} %projected_hbm.1, f32[3,3,1024]{2,1,0:T(4,128)} %short_filters.1, f32[512,1024]{1,0:T(8,128)} %long_filter_hbm.1, f32[1,1024]{1,0:T(1,128)} %bitcast.3, bf16[1024,4096]{1,0:T(8,128)(2,1)} %weight_hbm.1, ...), custom_call_target="tpu_custom_call" | custom-call | tf_op jit(solution)/shard_map/mixer/pallas_call | solution.py:587
  127.1 3.3 %add.1 = f32[512,1024]{1,0:T(8,128)} custom-call(f32[512,1024]{1,0:T(8,128)} %get-tuple-element.8.kept, f32[512,1024]{1,0:T(8,128)} %bitcast.2, f32[128,1024]{1,0:T(8,128)} %get-tuple-element.10.landed_chunk), custom_call_target="tpu_custom_call" | custom-call | tf_op jit(solution)/shard_map/add/pallas_call | solution.py:654
